TPU v7x, 32 devices: a whole 2x2x4 slice. The times are simulated.
32 devices in a mesh: dp: 8 (over z, x), ctx: 4 (over y, core).
Axes of the slice: x: 2, y: 2, z: 4, core: 2. Of those that a mesh axis runs over, the one named last changes fastest.
Arguments:
- tokens: bfloat16 [16, 1024, 1024], P('dp', 'ctx'), may hold values from -6 to 6
- doc_lengths: int32 [16, 3], P('dp'), may hold values from 1 to 1022, as said below
- in_gain: bfloat16 [1024], P(('dp', 'ctx')), may hold values from 0.25 to 1.75
- w_query: bfloat16 [1024, 2048], P(('dp', 'ctx')), may hold values from -0.1875 to 0.1875
- w_key: bfloat16 [1024, 1024], P(('dp', 'ctx')), may hold values from -0.1875 to 0.1875
- w_value: bfloat16 [1024, 1024], P(('dp', 'ctx')), may hold values from -0.1875 to 0.1875
- q_gain: bfloat16 [128], P(('dp', 'ctx')), may hold values from 0.25 to 1.75
- k_gain: bfloat16 [128], P(('dp', 'ctx')), may hold values from 0.25 to 1.75
- w_out: bfloat16 [2048, 1024], P(('dp', 'ctx')), may hold values from -1 to 1
- post_gain: bfloat16 [1024], P(('dp', 'ctx')), may hold values from 0.25 to 1.75
- w_gate: bfloat16 [1024, 3072], P(('dp', 'ctx')), may hold values from -0.1875 to 0.1875
- w_up: bfloat16 [1024, 3072], P(('dp', 'ctx')), may hold values from -0.1875 to 0.1875
- w_down: bfloat16 [3072, 1024], P(('dp', 'ctx')), may hold values from -0.109375 to 0.109375
- cotangent: bfloat16 [16, 1024, 1024], P('dp', 'ctx'), may hold values from -6 to 6
Outputs:
- mixed: bfloat16 [16, 1024, 1024], P('dp', 'ctx')
- tokens_grad: float32 [16, 1024, 1024], P('dp', 'ctx')
- in_gain_grad: float32 [1024], P(('dp', 'ctx'))
- w_query_grad: float32 [1024, 2048], P(('dp', 'ctx'))
- w_key_grad: float32 [1024, 1024], P(('dp', 'ctx'))
- w_value_grad: float32 [1024, 1024], P(('dp', 'ctx'))
- q_gain_grad: float32 [128], P(('dp', 'ctx'))
- k_gain_grad: float32 [128], P(('dp', 'ctx'))
- w_out_grad: float32 [2048, 1024], P(('dp', 'ctx'))
- post_gain_grad: float32 [1024], P(('dp', 'ctx'))
- w_gate_grad: float32 [1024, 3072], P(('dp', 'ctx'))
- w_up_grad: float32 [1024, 3072], P(('dp', 'ctx'))
- w_down_grad: float32 [3072, 1024], P(('dp', 'ctx'))
Inputs may be any that keep to these rules, and one draw needn't show every extreme that they name: `doc_lengths`: each row holds three document lengths that sum to 1024; the first and the last are each under 256, so the middle document holds tokens of every device along ctx.
All inputs are finite; a program needn't handle non-finite values.
Results may differ from a plain program's by a relative error of at most 0.02.
Values may be sent and summed in bfloat16 or wider, within the bound.
A program may use at most 256 MiB of HBM per device.

v0:
```python
import math

import jax
import jax.numpy as jnp
from jax import lax
from jax.sharding import PartitionSpec as P

EPSILON = 1e-06
THETA = 1000000.0
NEGATIVE = -1e30


def doc_layout(doc_lengths, positions):
    doc_ends = jnp.cumsum(doc_lengths, axis=1)
    passed = positions[None, :, None] >= doc_ends[:, None, :]
    segment = jnp.sum(passed.astype(jnp.int32), axis=2)
    doc_start = jnp.sum(jnp.where(passed, doc_lengths[:, None, :], 0), axis=2)
    return (segment, positions[None, :] - doc_start)


def rope_tables(relative, head_dim):
    half_dim = head_dim // 2
    exponent = jnp.arange(half_dim, dtype=jnp.float32) * (2.0 / head_dim)
    inverse = jnp.exp(-math.log(THETA) * exponent)
    angles = relative.astype(jnp.float32)[..., None] * inverse
    return (jnp.cos(angles), jnp.sin(angles))


def rotate(values, cosine_table, sine_table):
    half_dim = values.shape[-1] // 2
    front_part = values[..., :half_dim]
    back_part = values[..., half_dim:]
    return jnp.concatenate(
        [
            front_part * cosine_table - back_part * sine_table,
            back_part * cosine_table + front_part * sine_table,
        ],
        axis=-1,
    )


def unrotate(grads, cosine_table, sine_table):
    half_dim = grads.shape[-1] // 2
    front_part = grads[..., :half_dim]
    back_part = grads[..., half_dim:]
    return jnp.concatenate(
        [
            front_part * cosine_table + back_part * sine_table,
            back_part * cosine_table - front_part * sine_table,
        ],
        axis=-1,
    )


def norm_forward(values, gain):
    inverse = lax.rsqrt(jnp.mean(values * values, axis=-1, keepdims=True) + EPSILON)
    return (values * inverse * gain, inverse)


def norm_backward(values, inverse, gain, grad_out):
    scaled = grad_out * gain
    cubed = inverse * inverse * inverse
    value_grad = inverse * scaled - values * cubed * jnp.mean(
        scaled * values, axis=-1, keepdims=True
    )
    gain_grad = jnp.sum((grad_out * values * inverse).reshape(-1, values.shape[-1]), axis=0)
    return (value_grad, gain_grad)


def lead_product(left, right):
    return lax.dot_general(
        left, right, (((0,), (0,)), ((), ())), preferred_element_type=jnp.float32
    )


def tail_product(left, right):
    return lax.dot_general(
        left, right, (((1,), (1,)), ((), ())), preferred_element_type=jnp.float32
    )


def local(
    tokens,
    doc_lengths,
    in_gain,
    w_query,
    w_key,
    w_value,
    q_gain,
    k_gain,
    w_out,
    post_gain,
    w_gate,
    w_up,
    w_down,
    cotangent,
):
    attn_front = (
        lax.all_gather(in_gain, ("dp", "ctx"), axis=0, tiled=True),
        lax.all_gather(w_query, ("dp", "ctx"), axis=0, tiled=True),
        lax.all_gather(w_key, ("dp", "ctx"), axis=0, tiled=True),
        lax.all_gather(w_value, ("dp", "ctx"), axis=0, tiled=True),
        lax.all_gather(q_gain, ("dp", "ctx"), axis=0, tiled=True),
        lax.all_gather(k_gain, ("dp", "ctx"), axis=0, tiled=True),
        lax.all_gather(w_out, ("dp", "ctx"), axis=0, tiled=True),
    )
    mlp_front = (
        lax.all_gather(post_gain, ("dp", "ctx"), axis=0, tiled=True),
        lax.all_gather(w_gate, ("dp", "ctx"), axis=0, tiled=True),
        lax.all_gather(w_up, ("dp", "ctx"), axis=0, tiled=True),
        lax.all_gather(w_down, ("dp", "ctx"), axis=0, tiled=True),
    )
    gain_one, query_mat, key_mat, value_mat, qgain_full, kgain_full, out_mat = attn_front
    gain_two, gate_mat, up_mat, down_mat = mlp_front
    seq_count, local_len, model_width = tokens.shape
    seq_len = local_len * lax.axis_size("ctx")
    head_dim = qgain_full.shape[0]
    kv_heads = key_mat.shape[1] // head_dim
    q_heads = query_mat.shape[1] // head_dim
    group_size = q_heads // kv_heads
    kv_width = kv_heads * head_dim
    row_count = seq_count * local_len
    score_scale = head_dim ** (-0.5)
    local_pos = lax.axis_index("ctx") * local_len + jnp.arange(local_len, dtype=jnp.int32)
    key_pos = jnp.arange(seq_len, dtype=jnp.int32)
    q_segment, q_relative = doc_layout(doc_lengths, local_pos)
    k_segment = doc_layout(doc_lengths, key_pos)[0]
    gain_in = gain_one.astype(jnp.float32)
    gain_query = qgain_full.astype(jnp.float32)
    gain_key = kgain_full.astype(jnp.float32)
    gain_post = gain_two.astype(jnp.float32)
    inputs = tokens.reshape(row_count, model_width).astype(jnp.float32)
    normed, inverse_one = norm_forward(inputs, gain_in)
    normed_low = normed.astype(jnp.bfloat16)
    queries = jnp.dot(normed_low, query_mat, preferred_element_type=jnp.float32).reshape(
        seq_count, local_len, q_heads, head_dim
    )
    key_pre = jnp.dot(normed_low, key_mat, preferred_element_type=jnp.float32).reshape(
        seq_count, local_len, kv_heads, head_dim
    )
    values_low = (
        jnp.dot(normed_low, value_mat, preferred_element_type=jnp.float32)
        .astype(jnp.bfloat16)
        .reshape(seq_count, local_len, kv_width)
    )
    cosine_table, sine_table = rope_tables(q_relative, head_dim)
    cosine_table = cosine_table[:, :, None, :]
    sine_table = sine_table[:, :, None, :]
    q_normed, q_inverse = norm_forward(queries, gain_query)
    q_low = rotate(q_normed, cosine_table, sine_table).astype(jnp.bfloat16)
    k_normed, k_inverse = norm_forward(key_pre, gain_key)
    k_low = (
        rotate(k_normed, cosine_table, sine_table)
        .astype(jnp.bfloat16)
        .reshape(seq_count, local_len, kv_width)
    )
    key_all, value_all = (
        lax.all_gather(k_low, "ctx", axis=1, tiled=True),
        lax.all_gather(values_low, "ctx", axis=1, tiled=True),
    )

    def block_scores(q_seq, k_seq, q_seg, k_seg, k_positions):
        grouped = q_seq.reshape(local_len, kv_heads, group_size, head_dim)
        key_heads = k_seq.reshape(k_seq.shape[0], kv_heads, head_dim)
        scores = score_scale * jnp.einsum(
            "qkgd,skd->kgqs", grouped, key_heads, preferred_element_type=jnp.float32
        )
        allowed = (q_seg[:, None] == k_seg[None, :]) & (k_positions[None, :] <= local_pos[:, None])
        return (jnp.where(allowed, scores, NEGATIVE), grouped, key_heads)

    def attend(seq_item):
        q_seq, k_seq, v_seq, q_seg, k_seg = seq_item
        scores, grouped, key_heads = block_scores(q_seq, k_seq, q_seg, k_seg, key_pos)
        value_heads = v_seq.reshape(seq_len, kv_heads, head_dim)
        row_peak = jnp.max(scores, axis=-1, keepdims=True)
        exp_scores = jnp.exp(scores - row_peak)
        row_total = jnp.sum(exp_scores, axis=-1, keepdims=True)
        probs_low = (exp_scores / row_total).astype(jnp.bfloat16)
        attended = jnp.einsum(
            "kgqs,skd->qkgd", probs_low, value_heads, preferred_element_type=jnp.float32
        )
        return (
            attended.reshape(local_len, q_heads * head_dim).astype(jnp.bfloat16),
            row_peak + jnp.log(row_total),
        )

    attended, log_totals = lax.map(attend, (q_low, key_all, value_all, q_segment, k_segment))
    attended_flat = attended.reshape(row_count, q_heads * head_dim)
    resid = inputs + jnp.dot(attended_flat, out_mat, preferred_element_type=jnp.float32)
    normed_two, inverse_two = norm_forward(resid, gain_post)
    normed_two_low = normed_two.astype(jnp.bfloat16)
    gate_pre = jnp.dot(normed_two_low, gate_mat, preferred_element_type=jnp.float32)
    up_pre = jnp.dot(normed_two_low, up_mat, preferred_element_type=jnp.float32)
    gate_sigmoid = jax.nn.sigmoid(gate_pre)
    gate_silu = gate_pre * gate_sigmoid
    hidden_low = (gate_silu * up_pre).astype(jnp.bfloat16)
    mixed = (resid + jnp.dot(hidden_low, down_mat, preferred_element_type=jnp.float32)).astype(
        jnp.bfloat16
    )
    attn_back = (
        lax.all_gather(in_gain, ("dp", "ctx"), axis=0, tiled=True),
        lax.all_gather(w_query, ("dp", "ctx"), axis=0, tiled=True),
        lax.all_gather(w_key, ("dp", "ctx"), axis=0, tiled=True),
        lax.all_gather(w_value, ("dp", "ctx"), axis=0, tiled=True),
        lax.all_gather(q_gain, ("dp", "ctx"), axis=0, tiled=True),
        lax.all_gather(k_gain, ("dp", "ctx"), axis=0, tiled=True),
        lax.all_gather(w_out, ("dp", "ctx"), axis=0, tiled=True),
    )
    mlp_back = (
        lax.all_gather(post_gain, ("dp", "ctx"), axis=0, tiled=True),
        lax.all_gather(w_gate, ("dp", "ctx"), axis=0, tiled=True),
        lax.all_gather(w_up, ("dp", "ctx"), axis=0, tiled=True),
        lax.all_gather(w_down, ("dp", "ctx"), axis=0, tiled=True),
    )
    gain_one_b, query_back, key_back, value_back, qgain_b, kgain_b, out_back = attn_back
    gain_two_b, gate_back, up_back, down_back = mlp_back
    grad_low = cotangent.reshape(row_count, model_width)
    w_down_grad = lead_product(hidden_low, grad_low)
    hidden_grad = tail_product(grad_low, down_back)
    gate_grad = (
        hidden_grad * up_pre * gate_sigmoid * (1.0 + gate_pre * (1.0 - gate_sigmoid))
    ).astype(jnp.bfloat16)
    up_grad = (hidden_grad * gate_silu).astype(jnp.bfloat16)
    w_gate_grad = lead_product(normed_two_low, gate_grad)
    w_up_grad = lead_product(normed_two_low, up_grad)
    normed_two_grad = tail_product(gate_grad, gate_back) + tail_product(up_grad, up_back)
    resid_norm_grad, post_gain_grad = norm_backward(
        resid, inverse_two, gain_two_b.astype(jnp.float32), normed_two_grad
    )
    resid_grad = grad_low.astype(jnp.float32) + resid_norm_grad
    resid_low = resid_grad.astype(jnp.bfloat16)
    w_out_grad = lead_product(attended_flat, resid_low)
    attended_grad = (
        tail_product(resid_low, out_back)
        .astype(jnp.bfloat16)
        .reshape(seq_count, local_len, q_heads * head_dim)
    )

    def score_terms(q_seq, k_seq, v_seq, q_seg, k_seg, k_positions, log_total, grad_seq):
        scores, grouped, key_heads = block_scores(q_seq, k_seq, q_seg, k_seg, k_positions)
        value_heads = v_seq.reshape(k_seq.shape[0], kv_heads, head_dim)
        attn_probs = jnp.exp(scores - log_total)
        grad_heads = grad_seq.reshape(local_len, kv_heads, group_size, head_dim)
        prob_grad = jnp.einsum(
            "qkgd,skd->kgqs", grad_heads, value_heads, preferred_element_type=jnp.float32
        )
        return (attn_probs, prob_grad, grouped, key_heads, grad_heads)

    def attend_back(seq_item):
        q_seq, k_seq, v_seq, q_seg, k_seg, log_total, grad_seq = seq_item
        attn_probs, prob_grad, grouped, key_heads, grad_heads = score_terms(
            q_seq, k_seq, v_seq, q_seg, k_seg, key_pos, log_total, grad_seq
        )
        probs_low = attn_probs.astype(jnp.bfloat16)
        row_dot = jnp.sum(attn_probs * prob_grad, axis=-1, keepdims=True)
        score_grad = (attn_probs * (prob_grad - row_dot)).astype(jnp.bfloat16)
        query_grad = score_scale * jnp.einsum(
            "kgqs,skd->qkgd", score_grad, key_heads, preferred_element_type=jnp.float32
        )
        key_grad = score_scale * jnp.einsum(
            "kgqs,qkgd->skd", score_grad, grouped, preferred_element_type=jnp.float32
        )
        value_grad = jnp.einsum(
            "kgqs,qkgd->skd", probs_low, grad_heads, preferred_element_type=jnp.float32
        )
        return (
            query_grad.reshape(local_len, q_heads, head_dim),
            key_grad.reshape(seq_len, kv_width),
            value_grad.reshape(seq_len, kv_width),
        )

    q_rot_grad, key_grad_all, value_grad_all = lax.map(
        attend_back, (q_low, key_all, value_all, q_segment, k_segment, log_totals, attended_grad)
    )
    key_part, value_part = (
        lax.psum_scatter(
            key_grad_all.astype(jnp.bfloat16), "ctx", scatter_dimension=1, tiled=True
        ).astype(jnp.float32),
        lax.psum_scatter(
            value_grad_all.astype(jnp.bfloat16), "ctx", scatter_dimension=1, tiled=True
        ).astype(jnp.float32),
    )
    q_pre_grad, q_gain_grad = norm_backward(
        queries,
        q_inverse,
        qgain_b.astype(jnp.float32),
        unrotate(q_rot_grad, cosine_table, sine_table),
    )
    k_rot_grad = key_part.reshape(seq_count, local_len, kv_heads, head_dim)
    k_pre_grad, k_gain_grad = norm_backward(
        key_pre,
        k_inverse,
        kgain_b.astype(jnp.float32),
        unrotate(k_rot_grad, cosine_table, sine_table),
    )
    queries_grad = q_pre_grad.astype(jnp.bfloat16).reshape(row_count, q_heads * head_dim)
    keys_grad = k_pre_grad.astype(jnp.bfloat16).reshape(row_count, kv_width)
    values_low_grad = value_part.astype(jnp.bfloat16).reshape(row_count, kv_width)
    w_query_grad = lead_product(normed_low, queries_grad)
    w_key_grad = lead_product(normed_low, keys_grad)
    w_value_grad = lead_product(normed_low, values_low_grad)
    normed_grad = (
        tail_product(queries_grad, query_back)
        + tail_product(keys_grad, key_back)
        + tail_product(values_low_grad, value_back)
    )
    input_norm_grad, in_gain_grad = norm_backward(
        inputs, inverse_one, gain_one_b.astype(jnp.float32), normed_grad
    )
    tokens_grad = (resid_grad + input_norm_grad).reshape(seq_count, local_len, model_width)
    attn_grads = (
        lax.psum_scatter(in_gain_grad, ("dp", "ctx"), scatter_dimension=0, tiled=True),
        lax.psum_scatter(w_query_grad, ("dp", "ctx"), scatter_dimension=0, tiled=True),
        lax.psum_scatter(w_key_grad, ("dp", "ctx"), scatter_dimension=0, tiled=True),
        lax.psum_scatter(w_value_grad, ("dp", "ctx"), scatter_dimension=0, tiled=True),
        lax.psum_scatter(q_gain_grad, ("dp", "ctx"), scatter_dimension=0, tiled=True),
        lax.psum_scatter(k_gain_grad, ("dp", "ctx"), scatter_dimension=0, tiled=True),
        lax.psum_scatter(w_out_grad, ("dp", "ctx"), scatter_dimension=0, tiled=True),
    )
    mlp_grads = (
        lax.psum_scatter(post_gain_grad, ("dp", "ctx"), scatter_dimension=0, tiled=True),
        lax.psum_scatter(w_gate_grad, ("dp", "ctx"), scatter_dimension=0, tiled=True),
        lax.psum_scatter(w_up_grad, ("dp", "ctx"), scatter_dimension=0, tiled=True),
        lax.psum_scatter(w_down_grad, ("dp", "ctx"), scatter_dimension=0, tiled=True),
    )
    return (
        mixed.reshape(seq_count, local_len, model_width),
        tokens_grad,
        attn_grads[0],
        attn_grads[1],
        attn_grads[2],
        attn_grads[3],
        attn_grads[4],
        attn_grads[5],
        attn_grads[6],
        mlp_grads[0],
        mlp_grads[1],
        mlp_grads[2],
        mlp_grads[3],
    )


def solution(mesh):
    placed = (
        P("dp", "ctx", None),
        P("dp", None),
        P(("dp", "ctx")),
        P(("dp", "ctx"), None),
        P(("dp", "ctx"), None),
        P(("dp", "ctx"), None),
        P(("dp", "ctx")),
        P(("dp", "ctx")),
        P(("dp", "ctx"), None),
        P(("dp", "ctx")),
        P(("dp", "ctx"), None),
        P(("dp", "ctx"), None),
        P(("dp", "ctx"), None),
        P("dp", "ctx", None),
    )
    return jax.shard_map(
        local,
        mesh=mesh,
        in_specs=placed,
        out_specs=(
            P("dp", "ctx", None),
            P("dp", "ctx", None),
            P(("dp", "ctx")),
            P(("dp", "ctx"), None),
            P(("dp", "ctx"), None),
            P(("dp", "ctx"), None),
            P(("dp", "ctx")),
            P(("dp", "ctx")),
            P(("dp", "ctx"), None),
            P(("dp", "ctx")),
            P(("dp", "ctx"), None),
            P(("dp", "ctx"), None),
            P(("dp", "ctx"), None),
        ),
        check_vma=False,
    )
```

profile of v0, /device:TPU:0, one launch (start us, length us, event | category | flops | bytes accessed | tf_op | source)
XLA Modules:
  0.0 1868.3 jit_solution(4474334712910635939)
XLA Ops:
  12.9 42.2 %all-reduce.9 = (bf16[1024]{0:T(1024)(128)(2,1)S(1)}, bf16[128]{0:T(256)(128)(2,1)S(1)}, bf16[128]{0:T(256)(128)(2,1)S(1)}, bf16[1024]{0:T(1024)(128)(2,1)S(1)}) all-reduce(bf16[1024]{0:T(1024)(128)(2,1)S(1)} %dynamic-update-slice, bf16[128]{0:T(256)(128)(2,1)S(1)} %dynamic-update-slice.1, ...), channel_id=1, replica_groups=mesh['dp'=8,'ctx'=4] {'dp','ctx'}, use_global_device_ids=true, to_apply=%add | all-reduce | flops 2304 | bytes 9216
  57.1 13.0 all-gather.10.cloned.1.call-done
  76.7 51.6 %all-gather.14.cloned.1.call-done = bf16[1024,1024]{1,0:T(8,128)(2,1)} async-done(((bf16[32,1024]{1,0:T(8,128)(2,1)}), bf16[1024,1024]{1,0:T(8,128)(2,1)}) %all-gather.14.cloned.1.call-update) | async-done | bytes 2097168 | tf_op jit(solution)/shard_map/all_gather | solution.py:101
  138.9 53.1 %all-gather.18.cloned.1.call-done = bf16[1024,2048]{1,0:T(8,128)(2,1)} async-done(((bf16[32,2048]{1,0:T(8,128)(2,1)}), bf16[1024,2048]{1,0:T(8,128)(2,1)}) %all-gather.18.cloned.1.call-update) | async-done | bytes 4194320 | tf_op jit(solution)/shard_map/all_gather | solution.py:100
  211.4 16.3 all-gather.12.cloned.1.call-done
  227.6 36.5 %all-gather.16.cloned.1.call-done = bf16[2,1024,1024]{1,2,0:T(8,128)(2,1)} async-done(((bf16[2,256,1024]{1,2,0:T(8,128)(2,1)}), bf16[2,1024,1024]{1,2,0:T(8,128)(2,1)}) %all-gather.16.cloned.1.call-update) | async-done | bytes 4194320 | tf_op jit(solution)/shard_map/all_gather | solution.py:158
  264.1 64.0 %while.28 = (s32[]{:T(128)}, bf16[2,256,2048]{2,1,0:T(8,128)(2,1)}, f32[2,8,2,256,1]{3,2,1,4,0:T(2,128)S(1)}, bf16[2,1024,1024]{1,2,0:T(8,128)(2,1)}, s32[2,256]...) while((s32[]{:T(128)}, bf16[2,256,2048]{2,1,0:T(8,128)(2,1)}, ...), condition=%wide.region_10.11_spmd.clone, body=%wide.region_7.10_spmd.clone.sunk | while | flops 2199122176 | bytes 72500360 | solution.py:187
  274.9 9.2 fusion.138
  284.1 9.3 fusion.139
  306.4 9.7 fusion.138
  316.1 9.4 fusion.139
  336.0 64.0 %all-gather.22.cloned.1.call-done = bf16[1024,3072]{1,0:T(8,128)(2,1)} async-done(((bf16[32,3072]{1,0:T(8,128)(2,1)}), bf16[1024,3072]{1,0:T(8,128)(2,1)}) %all-gather.22.cloned.1.call-update) | async-done | bytes 6291472 | tf_op jit(solution)/shard_map/all_gather | solution.py:109
  400.0 17.9 fusion.59
  417.9 53.1 %all-gather.24.cloned.1.call-done = bf16[1024,3072]{1,0:T(8,128)(2,1)} async-done(((bf16[32,3072]{1,0:T(8,128)(2,1)}), bf16[1024,3072]{1,0:T(8,128)(2,1)}) %all-gather.24.cloned.1.call-update) | async-done | bytes 6291472 | tf_op jit(solution)/shard_map/all_gather | solution.py:110
  480.2 61.9 %all-gather.26.cloned.1.call-done = bf16[3072,1024]{1,0:T(8,128)(2,1)} async-done(((bf16[96,1024]{1,0:T(8,128)(2,1)}), bf16[3072,1024]{1,0:T(8,128)(2,1)}) %all-gather.26.cloned.1.call-update) | async-done | bytes 6291472 | tf_op jit(solution)/shard_map/all_gather | solution.py:111
  542.0 11.5 multiply_convert_fusion
  571.7 134.8 %while.29 = (s32[]{:T(128)}, f32[2,256,16,128]{1,3,2,0:T(8,128)}, bf16[2,1024,1024]{1,2,0:T(8,128)(2,1)}, bf16[2,1024,1024]{2,1,0:T(8,128)(2,1)}, bf16[2,1024,10...) while((s32[]{:T(128)}, f32[2,256,16,128]{1,3,2,0:T(8,128)}, ...), condition=%wide.region_15.16_spmd.clone, body=%wide.region_13.15_spmd.clone.sunk | while | flops 5409861632 | bytes 266962288 | solution.py:272
  580.2 9.8 fusion.150
  591.7 12.0 fusion.152
  603.7 11.5 fusion.153
  647.3 9.8 fusion.150
  658.8 12.0 fusion.152
  670.8 11.5 fusion.153
  774.2 22.7 %reduce-scatter.12.cloned.1.call-done = bf16[2,256,1024]{2,1,0:T(8,128)(2,1)} async-done(((bf16[2,1024,1024]{2,1,0:T(8,128)(2,1)}), bf16[2,256,1024]{2,1,0:T(8,128)(2,1)}) %reduce-scatter.12.cloned.1.call-update) | async-done | bytes 1048592 | tf_op jit(solution)/shard_map/reduce_scatter | solution.py:279
  820.1 41.8 %all-reduce.8 = (f32[1024]{0:T(1024)S(1)}, f32[128]{0:T(128)S(1)}, f32[128]{0:T(128)S(1)}, f32[1024]{0:T(1024)S(1)}) all-reduce(f32[1024]{0:T(1024)S(1)} %get-tuple-element.280, f32[128]{0:T(128)S(1)} %get-tuple-element.274, f32[128]{0:T(128)S(1)} %get-tuple-element.278, ...), channel_id=4, replica_groups=mesh['dp'=8,'ctx'=4] {'dp','ctx'}, use_global_device_ids=true, to_apply=%region_22.23.clone | all-reduce | flops 2304 | bytes 18432
  867.7 81.1 %reduce-scatter.14.cloned.1.call-done = f32[32,2048]{1,0:T(8,128)} async-done(((f32[1024,2048]{1,0:T(8,128)}), f32[32,2048]{1,0:T(8,128)}) %reduce-scatter.14.cloned.1.call-update) | async-done | bytes 262160 | tf_op jit(solution)/shard_map/reduce_scatter | solution.py:313
  948.8 147.7 %reduce-scatter.20.cloned.1.call-done = f32[64,1024]{1,0:T(8,128)} async-done(((f32[2048,1024]{1,0:T(8,128)}), f32[64,1024]{1,0:T(8,128)}) %reduce-scatter.20.cloned.1.call-update) | async-done | bytes 262160 | tf_op jit(solution)/shard_map/reduce_scatter | solution.py:318
  1096.5 158.1 %reduce-scatter.22.cloned.1.call-done = f32[32,3072]{1,0:T(8,128)} async-done(((f32[1024,3072]{1,0:T(8,128)}), f32[32,3072]{1,0:T(8,128)}) %reduce-scatter.22.cloned.1.call-update) | async-done | bytes 393232 | tf_op jit(solution)/shard_map/reduce_scatter | solution.py:322
  1254.6 162.3 %reduce-scatter.24.cloned.1.call-done = f32[32,3072]{1,0:T(8,128)} async-done(((f32[1024,3072]{1,0:T(8,128)}), f32[32,3072]{1,0:T(8,128)}) %reduce-scatter.24.cloned.1.call-update) | async-done | bytes 393232 | tf_op jit(solution)/shard_map/reduce_scatter | solution.py:323
  1417.0 160.9 %reduce-scatter.26.cloned.1.call-done = f32[96,1024]{1,0:T(8,128)} async-done(((f32[3072,1024]{1,0:T(8,128)}), f32[96,1024]{1,0:T(8,128)}) %reduce-scatter.26.cloned.1.call-update) | async-done | bytes 393232 | tf_op jit(solution)/shard_map/reduce_scatter | solution.py:324
  1577.9 143.1 %reduce-scatter.16.cloned.1.call-done = f32[32,1024]{1,0:T(8,128)} async-done(((f32[1024,1024]{1,0:T(8,128)}), f32[32,1024]{1,0:T(8,128)}) %reduce-scatter.16.cloned.1.call-update) | async-done | bytes 131088 | tf_op jit(solution)/shard_map/reduce_scatter | solution.py:314
  1721.0 140.0 %reduce-scatter.18.cloned.1.call-done = f32[32,1024]{1,0:T(8,128)} async-done(((f32[1024,1024]{1,0:T(8,128)}), f32[32,1024]{1,0:T(8,128)}) %reduce-scatter.18.cloned.1.call-update) | async-done | bytes 131088 | tf_op jit(solution)/shard_map/reduce_scatter | solution.py:315
  (298 shorter events, 268.6 us)
Async XLA Ops:
  7.2 49.4 %copy-start.4 = (bf16[2,256,1024]{2,1,0:T(8,128)(2,1)S(1)}, bf16[2,256,1024]{2,1,0:T(8,128)(2,1)}, u32[]{:S(2)}) copy-start(bf16[2,256,1024]{2,1,0:T(8,128)(2,1)} %param.18) | copy-start | bytes 3145732
  7.2 62.9 %all-gather.10.cloned.1.call-start = ((), (), s32[]{:S(2)}) async-start(), calls=%async_computation.9 | async-start | bytes 2162688 | tf_op jit(solution)/shard_map/all_gather | solution.py:102
  7.9 120.3 %all-gather.14.cloned.1.call-start = ((), (), s32[]{:S(2)}) async-start(), calls=%async_computation.11 | async-start | bytes 2162688 | tf_op jit(solution)/shard_map/all_gather | solution.py:101
  8.7 183.4 %all-gather.18.cloned.1.call-start = ((), (), s32[]{:S(2)}) async-start(), calls=%async_computation.13 | async-start | bytes 4325376 | tf_op jit(solution)/shard_map/all_gather | solution.py:100
  9.4 218.2 %all-gather.12.cloned.1.call-start = ((), (), s32[]{:S(2)}) async-start(), calls=%async_computation.10 | async-start | bytes 5242880 | tf_op jit(solution)/shard_map/all_gather | solution.py:159
  55.1 20.3 %copy-start.38 = (f32[1024]{0:T(1024)}, f32[1024]{0:T(1024)S(1)}, u32[]{:S(2)}) copy-start(f32[1024]{0:T(1024)S(1)} %convert_element_type.131) | copy-start | bytes 12292
  74.3 189.8 %all-gather.16.cloned.1.call-start = ((), (), s32[]{:S(2)}) async-start(), calls=%async_computation.12 | async-start | bytes 5242880 | tf_op jit(solution)/shard_map/all_gather | solution.py:158
  74.7 58.5 %copy-start.44 = (f32[128]{0:T(128)}, f32[128]{0:T(128)S(1)}, u32[]{:S(2)}) copy-start(f32[128]{0:T(128)S(1)} %convert_element_type.137) | copy-start | bytes 1540
  75.4 130.7 %copy-start.18 = (f32[2,256,64]{1,2,0:T(8,128)}, f32[2,256,64]{1,2,0:T(8,128)S(1)}, u32[]{:S(2)}) copy-start(f32[2,256,64]{1,2,0:T(8,128)S(1)} %get-tuple-element.357) | copy-start | bytes 393220
  75.4 130.7 %copy-start.20 = (f32[2,256,64]{1,2,0:T(8,128)}, f32[2,256,64]{1,2,0:T(8,128)S(1)}, u32[]{:S(2)}) copy-start(f32[2,256,64]{1,2,0:T(8,128)S(1)} %get-tuple-element.358) | copy-start | bytes 393220
  135.3 193.6 %all-gather.20.cloned.1.call-start = ((), (), s32[]{:S(2)}) async-start(), calls=%async_computation.14 | async-start | bytes 4325376 | tf_op jit(solution)/shard_map/all_gather | solution.py:105
  135.9 264.1 %all-gather.22.cloned.1.call-start = ((), (), s32[]{:S(2)}) async-start(), calls=%async_computation.15 | async-start | bytes 6488064 | tf_op jit(solution)/shard_map/all_gather | solution.py:109
  136.6 334.4 %all-gather.24.cloned.1.call-start = ((), (), s32[]{:S(2)}) async-start(), calls=%async_computation.16 | async-start | bytes 6488064 | tf_op jit(solution)/shard_map/all_gather | solution.py:110
  137.4 404.7 %all-gather.26.cloned.1.call-start = ((), (), s32[]{:S(2)}) async-start(), calls=%async_computation.17 | async-start | bytes 6488064 | tf_op jit(solution)/shard_map/all_gather | solution.py:111
  138.1 624.8 %reduce-scatter.10.cloned.1.call-start = ((), (), s32[]{:S(2)}) async-start(), calls=%async_computation.18 | async-start | bytes 5242880 | tf_op jit(solution)/shard_map/reduce_scatter | solution.py:276
  138.3 65.9 %copy-start.46 = (f32[128]{0:T(128)}, f32[128]{0:T(128)S(1)}, u32[]{:S(2)}) copy-start(f32[128]{0:T(128)S(1)} %convert_element_type.140) | copy-start | bytes 1540
  336.0 64.0 %copy-start.29 = (bf16[512,1024]{1,0:T(8,128)(2,1)}, bf16[512,1024]{1,0:T(8,128)(2,1)S(1)}, u32[]{:S(2)}) copy-start(bf16[512,1024]{1,0:T(8,128)(2,1)S(1)} %multiply_convert_fusion.3) | copy-start | bytes 3145732
  417.9 124.1 %copy-start.24 = (bf16[2,256,1024]{2,1,0:T(8,128)(2,1)S(1)}, bf16[2,256,1024]{2,1,0:T(8,128)(2,1)}, u32[]{:S(2)}) copy-start(bf16[2,256,1024]{2,1,0:T(8,128)(2,1)} %param.31) | copy-start | bytes 3145732
  553.5 7.9 copy-start.53
  553.5 7.9 copy-start.52
  553.5 7.9 copy-start.12
  553.5 7.9 copy-start.50
  706.5 90.4 %reduce-scatter.12.cloned.1.call-start = ((), (), s32[]{:S(2)}) async-start(), calls=%async_computation.19 | async-start | bytes 5242880 | tf_op jit(solution)/shard_map/reduce_scatter | solution.py:279
  707.3 241.6 %reduce-scatter.14.cloned.1.call-start = ((), (), s32[]{:S(2)}) async-start(), calls=%async_computation.20 | async-start | bytes 8650752 | tf_op jit(solution)/shard_map/reduce_scatter | solution.py:313
  725.6 370.9 %reduce-scatter.20.cloned.1.call-start = ((), (), s32[]{:S(2)}) async-start(), calls=%async_computation.23 | async-start | bytes 8650752 | tf_op jit(solution)/shard_map/reduce_scatter | solution.py:318
  734.5 520.1 %reduce-scatter.22.cloned.1.call-start = ((), (), s32[]{:S(2)}) async-start(), calls=%async_computation.24 | async-start | bytes 12976128 | tf_op jit(solution)/shard_map/reduce_scatter | solution.py:322
  743.9 673.1 %reduce-scatter.24.cloned.1.call-start = ((), (), s32[]{:S(2)}) async-start(), calls=%async_computation.25 | async-start | bytes 12976128 | tf_op jit(solution)/shard_map/reduce_scatter | solution.py:323
  752.4 825.4 %reduce-scatter.26.cloned.1.call-start = ((), (), s32[]{:S(2)}) async-start(), calls=%async_computation.26 | async-start | bytes 12976128 | tf_op jit(solution)/shard_map/reduce_scatter | solution.py:324
  762.8 958.2 %reduce-scatter.16.cloned.1.call-start = ((), (), s32[]{:S(2)}) async-start(), calls=%async_computation.21 | async-start | bytes 4325376 | tf_op jit(solution)/shard_map/reduce_scatter | solution.py:314
  773.9 23.1 %copy-start.28 = (bf16[2,256,1024]{2,1,0:T(8,128)(2,1)S(1)}, bf16[2,256,1024]{2,1,0:T(8,128)(2,1)}, u32[]{:S(2)}) copy-start(bf16[2,256,1024]{2,1,0:T(8,128)(2,1)} %fusion.30) | copy-start | bytes 3145732
  773.9 1087.1 %reduce-scatter.18.cloned.1.call-start = ((), (), s32[]{:S(2)}) async-start(), calls=%async_computation.22 | async-start | bytes 4325376 | tf_op jit(solution)/shard_map/reduce_scatter | solution.py:315
  807.4 7.3 copy-start.22
  (48 other events, 118.6 us)
Sparse Core Ops, SparseCore 0:
  10.9 59.1 all-gather.9
  72.9 55.2 all-gather.13
  131.1 60.8 all-gather.17
  194.0 33.5 all-gather.11
  229.0 35.0 all-gather.15
  266.8 62.0 all-gather.19
  331.8 68.1 all-gather.21
  402.9 68.0 all-gather.23
  473.9 68.0 all-gather.25
  706.6 43.0 reduce-scatter.9
  752.4 44.4 reduce-scatter.11
  799.6 149.1 reduce-scatter.13
  951.7 144.7 reduce-scatter.19
  1103.0 151.5 reduce-scatter.21
  1262.1 154.8 reduce-scatter.23
  1423.4 154.4 reduce-scatter.25
  1580.7 140.3 reduce-scatter.15
  1723.8 137.1 reduce-scatter.17
where the time goes:
time: 1880 us; the launch traced here: 1870 us
  waiting for transfers between devices  1370 us (73%)
  matrix products  239 us (13%)
  local copies, waits for them, and re-layouts  88.6 us (5%)
  blocking collectives  84.1 us (4%)
  other arithmetic  67.6 us (4%)
    reduce_scatter x1, waiting for transfers between devices, local(): lax.psum_scatter(w_up_grad, ('dp', 'ctx'), scatter_dimension=0, tiled=True)  162 us
    reduce_scatter x1, waiting for transfers between devices, local(): lax.psum_scatter(w_down_grad, ('dp', 'ctx'), scatter_dimension=0, tiled=T...  161 us
    reduce_scatter x1, waiting for transfers between devices, local(): lax.psum_scatter(w_gate_grad, ('dp', 'ctx'), scatter_dimension=0, tiled=T...  158 us
    reduce_scatter x1, waiting for transfers between devices, local(): lax.psum_scatter(w_out_grad, ('dp', 'ctx'), scatter_dimension=0, tiled=True)  148 us
    reduce_scatter x1, waiting for transfers between devices, local(): lax.psum_scatter(w_key_grad, ('dp', 'ctx'), scatter_dimension=0, tiled=True)  143 us
    reduce_scatter x1, waiting for transfers between devices, local(): lax.psum_scatter(w_value_grad, ('dp', 'ctx'), scatter_dimension=0, tiled=...  140 us
    unnamed x2, blocking collectives  84.1 us
    reduce_scatter x1, waiting for transfers between devices, local(): lax.psum_scatter(w_query_grad, ('dp', 'ctx'), scatter_dimension=0, tiled=...  81.1 us
  transfers between devices with their start and end apart: 18, of which 17 were waited for; matrix products, arithmetic and copies ran while one was open for 12% of the time, Pallas kernels for 0%

commit v1 on v0

--- a/solution.py
+++ b/solution.py
@@ -77,6 +77,64 @@
     return lax.dot_general(
         left, right, (((1,), (1,)), ((), ())), preferred_element_type=jnp.float32
     )
+
+
+AXES = ("dp", "ctx")
+
+
+def bit_orders(count):
+    bits = count.bit_length() - 1
+    rest = list(range(1, bits))
+    shift = max(1, (bits - 1) // 3)
+    return [[0] + rest[shift * turn :] + rest[: shift * turn] for turn in range(3)]
+
+
+def swap(block, axes, count, bit):
+    pairs = [(device, device ^ (1 << bit)) for device in range(count)]
+    return lax.ppermute(block, axes, pairs)
+
+
+def scatter_sum(terms, axes, order, lead=1, out_type=jnp.float32):
+    count = lax.axis_size(axes)
+    me = lax.axis_index(axes)
+    tail = (terms.shape[0] // (lead * count),) + terms.shape[1:]
+    left = sorted(order, reverse=True)
+    for step, bit in enumerate(order):
+        place = left.index(bit)
+        above = lead << place
+        below = 1 << (len(left) - place - 1)
+        left.remove(bit)
+        split = terms.reshape((above, 2, below * tail[0]) + tail[1:])
+        mine = (me >> bit) & 1
+        away = lax.dynamic_index_in_dim(split, 1 - mine, 1, keepdims=False)
+        keep = lax.dynamic_index_in_dim(split, mine, 1, keepdims=False)
+        got = swap(away, axes, count, bit)
+        total = keep.astype(jnp.float32) + got.astype(jnp.float32)
+        terms = total.astype(out_type if step == len(order) - 1 else terms.dtype)
+    return terms.reshape((lead * tail[0],) + tail[1:])
+
+
+def gather_all(shard, axes, order, lead=1):
+    count = lax.axis_size(axes)
+    me = lax.axis_index(axes)
+    tail = (shard.shape[0] // lead,) + shard.shape[1:]
+    held = []
+    block = shard
+    for bit in reversed(order):
+        got = swap(block, axes, count, bit)
+        mine = (me >> bit) & 1
+        held = sorted(held + [bit], reverse=True)
+        place = held.index(bit)
+        above = lead << place
+        below = 1 << (len(held) - place - 1)
+        shape = (above, 1, below * tail[0]) + tail[1:]
+        own = block.reshape(shape)
+        other = got.reshape(shape)
+        first = jnp.where(mine == 0, own, other)
+        second = jnp.where(mine == 0, other, own)
+        block = jnp.concatenate([first, second], axis=1)
+        block = block.reshape((lead * tail[0] << len(held),) + tail[1:])
+    return block
 
 
 def local(
@@ -95,23 +153,25 @@
     w_down,
     cotangent,
 ):
-    attn_front = (
-        lax.all_gather(in_gain, ("dp", "ctx"), axis=0, tiled=True),
-        lax.all_gather(w_query, ("dp", "ctx"), axis=0, tiled=True),
-        lax.all_gather(w_key, ("dp", "ctx"), axis=0, tiled=True),
-        lax.all_gather(w_value, ("dp", "ctx"), axis=0, tiled=True),
-        lax.all_gather(q_gain, ("dp", "ctx"), axis=0, tiled=True),
-        lax.all_gather(k_gain, ("dp", "ctx"), axis=0, tiled=True),
-        lax.all_gather(w_out, ("dp", "ctx"), axis=0, tiled=True),
-    )
-    mlp_front = (
-        lax.all_gather(post_gain, ("dp", "ctx"), axis=0, tiled=True),
-        lax.all_gather(w_gate, ("dp", "ctx"), axis=0, tiled=True),
-        lax.all_gather(w_up, ("dp", "ctx"), axis=0, tiled=True),
-        lax.all_gather(w_down, ("dp", "ctx"), axis=0, tiled=True),
-    )
-    gain_one, query_mat, key_mat, value_mat, qgain_full, kgain_full, out_mat = attn_front
-    gain_two, gate_mat, up_mat, down_mat = mlp_front
+    count = lax.axis_size(AXES)
+    orders = bit_orders(count)
+    ctx_order = list(range(lax.axis_size("ctx").bit_length() - 1))
+    gains = jnp.concatenate([in_gain, q_gain, k_gain, post_gain])
+    gain_width = -(-gains.shape[0] // 128) * 128
+    gains = jnp.pad(gains, (0, gain_width - gains.shape[0]))
+    gains = gather_all(gains[None, :], AXES, orders[0])
+    cuts = [in_gain.shape[0], q_gain.shape[0], k_gain.shape[0], post_gain.shape[0]]
+    ends = [sum(cuts[: i + 1]) for i in range(4)]
+    gain_one, qgain_full, kgain_full, gain_two = [
+        gains[:, end - cut : end].reshape(-1) for cut, end in zip(cuts, ends)
+    ]
+    query_mat = gather_all(w_query, AXES, orders[1])
+    key_mat = gather_all(w_key, AXES, orders[2])
+    value_mat = gather_all(w_value, AXES, orders[0])
+    out_mat = gather_all(w_out, AXES, orders[0])
+    gate_mat = gather_all(w_gate, AXES, orders[1])
+    up_mat = gather_all(w_up, AXES, orders[2])
+    down_mat = gather_all(w_down, AXES, orders[0])
     seq_count, local_len, model_width = tokens.shape
     seq_len = local_len * lax.axis_size("ctx")
     head_dim = qgain_full.shape[0]
@@ -154,10 +214,8 @@
         .astype(jnp.bfloat16)
         .reshape(seq_count, local_len, kv_width)
     )
-    key_all, value_all = (
-        lax.all_gather(k_low, "ctx", axis=1, tiled=True),
-        lax.all_gather(values_low, "ctx", axis=1, tiled=True),
-    )
+    key_all = [gather_all(k_low[i], "ctx", ctx_order) for i in range(seq_count)]
+    value_all = [gather_all(values_low[i], "ctx", ctx_order) for i in range(seq_count)]
 
     def block_scores(q_seq, k_seq, q_seg, k_seg, k_positions):
         grouped = q_seq.reshape(local_len, kv_heads, group_size, head_dim)
@@ -184,8 +242,12 @@
             row_peak + jnp.log(row_total),
         )
 
-    attended, log_totals = lax.map(attend, (q_low, key_all, value_all, q_segment, k_segment))
-    attended_flat = attended.reshape(row_count, q_heads * head_dim)
+    forward = [
+        attend((q_low[i], key_all[i], value_all[i], q_segment[i], k_segment[i]))
+        for i in range(seq_count)
+    ]
+    log_totals = [item[1] for item in forward]
+    attended_flat = jnp.concatenate([item[0] for item in forward], axis=0)
     resid = inputs + jnp.dot(attended_flat, out_mat, preferred_element_type=jnp.float32)
     normed_two, inverse_two = norm_forward(resid, gain_post)
     normed_two_low = normed_two.astype(jnp.bfloat16)
@@ -197,41 +259,24 @@
     mixed = (resid + jnp.dot(hidden_low, down_mat, preferred_element_type=jnp.float32)).astype(
         jnp.bfloat16
     )
-    attn_back = (
-        lax.all_gather(in_gain, ("dp", "ctx"), axis=0, tiled=True),
-        lax.all_gather(w_query, ("dp", "ctx"), axis=0, tiled=True),
-        lax.all_gather(w_key, ("dp", "ctx"), axis=0, tiled=True),
-        lax.all_gather(w_value, ("dp", "ctx"), axis=0, tiled=True),
-        lax.all_gather(q_gain, ("dp", "ctx"), axis=0, tiled=True),
-        lax.all_gather(k_gain, ("dp", "ctx"), axis=0, tiled=True),
-        lax.all_gather(w_out, ("dp", "ctx"), axis=0, tiled=True),
-    )
-    mlp_back = (
-        lax.all_gather(post_gain, ("dp", "ctx"), axis=0, tiled=True),
-        lax.all_gather(w_gate, ("dp", "ctx"), axis=0, tiled=True),
-        lax.all_gather(w_up, ("dp", "ctx"), axis=0, tiled=True),
-        lax.all_gather(w_down, ("dp", "ctx"), axis=0, tiled=True),
-    )
-    gain_one_b, query_back, key_back, value_back, qgain_b, kgain_b, out_back = attn_back
-    gain_two_b, gate_back, up_back, down_back = mlp_back
     grad_low = cotangent.reshape(row_count, model_width)
     w_down_grad = lead_product(hidden_low, grad_low)
-    hidden_grad = tail_product(grad_low, down_back)
+    hidden_grad = tail_product(grad_low, down_mat)
     gate_grad = (
         hidden_grad * up_pre * gate_sigmoid * (1.0 + gate_pre * (1.0 - gate_sigmoid))
     ).astype(jnp.bfloat16)
     up_grad = (hidden_grad * gate_silu).astype(jnp.bfloat16)
     w_gate_grad = lead_product(normed_two_low, gate_grad)
     w_up_grad = lead_product(normed_two_low, up_grad)
-    normed_two_grad = tail_product(gate_grad, gate_back) + tail_product(up_grad, up_back)
+    normed_two_grad = tail_product(gate_grad, gate_mat) + tail_product(up_grad, up_mat)
     resid_norm_grad, post_gain_grad = norm_backward(
-        resid, inverse_two, gain_two_b.astype(jnp.float32), normed_two_grad
+        resid, inverse_two, gain_two.astype(jnp.float32), normed_two_grad
     )
     resid_grad = grad_low.astype(jnp.float32) + resid_norm_grad
     resid_low = resid_grad.astype(jnp.bfloat16)
     w_out_grad = lead_product(attended_flat, resid_low)
     attended_grad = (
-        tail_product(resid_low, out_back)
+        tail_product(resid_low, out_mat)
         .astype(jnp.bfloat16)
         .reshape(seq_count, local_len, q_heads * head_dim)
     )
@@ -269,28 +314,38 @@
             value_grad.reshape(seq_len, kv_width),
         )
 
-    q_rot_grad, key_grad_all, value_grad_all = lax.map(
-        attend_back, (q_low, key_all, value_all, q_segment, k_segment, log_totals, attended_grad)
-    )
-    key_part, value_part = (
-        lax.psum_scatter(
-            key_grad_all.astype(jnp.bfloat16), "ctx", scatter_dimension=1, tiled=True
-        ).astype(jnp.float32),
-        lax.psum_scatter(
-            value_grad_all.astype(jnp.bfloat16), "ctx", scatter_dimension=1, tiled=True
-        ).astype(jnp.float32),
-    )
+    backward = [
+        attend_back(
+            (
+                q_low[i],
+                key_all[i],
+                value_all[i],
+                q_segment[i],
+                k_segment[i],
+                log_totals[i],
+                attended_grad[i],
+            )
+        )
+        for i in range(seq_count)
+    ]
+    q_rot_grad = jnp.stack([item[0] for item in backward])
+    key_part, value_part = [
+        jnp.stack(
+            [scatter_sum(item[j].astype(jnp.bfloat16), "ctx", ctx_order) for item in backward]
+        )
+        for j in (1, 2)
+    ]
     q_pre_grad, q_gain_grad = norm_backward(
         queries,
         q_inverse,
-        qgain_b.astype(jnp.float32),
+        qgain_full.astype(jnp.float32),
         unrotate(q_rot_grad, cosine_table, sine_table),
     )
     k_rot_grad = key_part.reshape(seq_count, local_len, kv_heads, head_dim)
     k_pre_grad, k_gain_grad = norm_backward(
         key_pre,
         k_inverse,
-        kgain_b.astype(jnp.float32),
+        kgain_full.astype(jnp.float32),
         unrotate(k_rot_grad, cosine_table, sine_table),
     )
     queries_grad = q_pre_grad.astype(jnp.bfloat16).reshape(row_count, q_heads * head_dim)
@@ -300,43 +355,40 @@
     w_key_grad = lead_product(normed_low, keys_grad)
     w_value_grad = lead_product(normed_low, values_low_grad)
     normed_grad = (
-        tail_product(queries_grad, query_back)
-        + tail_product(keys_grad, key_back)
-        + tail_product(values_low_grad, value_back)
+        tail_product(queries_grad, query_mat)
+        + tail_product(keys_grad, key_mat)
+        + tail_product(values_low_grad, value_mat)
     )
     input_norm_grad, in_gain_grad = norm_backward(
-        inputs, inverse_one, gain_one_b.astype(jnp.float32), normed_grad
+        inputs, inverse_one, gain_one.astype(jnp.float32), normed_grad
     )
     tokens_grad = (resid_grad + input_norm_grad).reshape(seq_count, local_len, model_width)
-    attn_grads = (
-        lax.psum_scatter(in_gain_grad, ("dp", "ctx"), scatter_dimension=0, tiled=True),
-        lax.psum_scatter(w_query_grad, ("dp", "ctx"), scatter_dimension=0, tiled=True),
-        lax.psum_scatter(w_key_grad, ("dp", "ctx"), scatter_dimension=0, tiled=True),
-        lax.psum_scatter(w_value_grad, ("dp", "ctx"), scatter_dimension=0, tiled=True),
-        lax.psum_scatter(q_gain_grad, ("dp", "ctx"), scatter_dimension=0, tiled=True),
-        lax.psum_scatter(k_gain_grad, ("dp", "ctx"), scatter_dimension=0, tiled=True),
-        lax.psum_scatter(w_out_grad, ("dp", "ctx"), scatter_dimension=0, tiled=True),
-    )
-    mlp_grads = (
-        lax.psum_scatter(post_gain_grad, ("dp", "ctx"), scatter_dimension=0, tiled=True),
-        lax.psum_scatter(w_gate_grad, ("dp", "ctx"), scatter_dimension=0, tiled=True),
-        lax.psum_scatter(w_up_grad, ("dp", "ctx"), scatter_dimension=0, tiled=True),
-        lax.psum_scatter(w_down_grad, ("dp", "ctx"), scatter_dimension=0, tiled=True),
-    )
+    gain_terms = jnp.concatenate(
+        [
+            part.reshape(count, -1)
+            for part in (in_gain_grad, q_gain_grad, k_gain_grad, post_gain_grad)
+        ],
+        axis=1,
+    )
+    gain_terms = jnp.pad(gain_terms, ((0, 0), (0, gain_width - gain_terms.shape[1])))
+    gain_sums = scatter_sum(gain_terms, AXES, orders[0])[0]
+    in_gain_sum, q_gain_sum, k_gain_sum, post_gain_sum = [
+        gain_sums[end - cut : end] for cut, end in zip(cuts, ends)
+    ]
     return (
         mixed.reshape(seq_count, local_len, model_width),
         tokens_grad,
-        attn_grads[0],
-        attn_grads[1],
-        attn_grads[2],
-        attn_grads[3],
-        attn_grads[4],
-        attn_grads[5],
-        attn_grads[6],
-        mlp_grads[0],
-        mlp_grads[1],
-        mlp_grads[2],
-        mlp_grads[3],
+        in_gain_sum,
+        scatter_sum(w_query_grad.astype(jnp.bfloat16), AXES, orders[1]),
+        scatter_sum(w_key_grad.astype(jnp.bfloat16), AXES, orders[2]),
+        scatter_sum(w_value_grad.astype(jnp.bfloat16), AXES, orders[0]),
+        q_gain_sum,
+        k_gain_sum,
+        scatter_sum(w_out_grad.astype(jnp.bfloat16), AXES, orders[0]),
+        post_gain_sum,
+        scatter_sum(w_gate_grad.astype(jnp.bfloat16), AXES, orders[1]),
+        scatter_sum(w_up_grad.astype(jnp.bfloat16), AXES, orders[2]),
+        scatter_sum(w_down_grad.astype(jnp.bfloat16), AXES, orders[0]),
     )
 
 

time: 1880 us -> 940 us (0.50)
  waiting for transfers between devices: 1370 us -> 314 us
  starting transfers between devices: 0.97 us -> 98.3 us
  local copies, waits for them, and re-layouts: 88.6 us -> 180 us
  blocking collectives: 84.1 us -> 0 us
  other arithmetic: 67.6 us -> 141 us
  matrix products: 239 us -> 192 us
    reduce_scatter x9 -> x0, waiting for transfers between devices: 1020 us -> none  [the longest x1 162 us: local(): lax.psum_scatter(w_up_grad, ('dp', 'ctx'), scatter_dimension=0, tiled=True)]
    all_gather x9 -> x0, waiting for transfers between devices: 350 us -> none  [the longest x1 64 us: local(): lax.all_gather(w_gate, ('dp', 'ctx'), axis=0, tiled=True)]
    ppermute x0 -> x96, waiting for transfers between devices: none -> 314 us  [swap(): return lax.ppermute(block, axes, pairs)]
    ppermute x0 -> x96, starting transfers between devices: none -> 98.3 us  [swap(): return lax.ppermute(block, axes, pairs)]
    unnamed x2 -> x0, blocking collectives: 84.1 us -> none
    select_n x0 -> x46, other arithmetic: none -> 29.2 us  [gather_all(): first = jnp.where(mine == 0, own, other)]
    convert_element_type x2 -> x32, other arithmetic: 0.01 us -> 29.2 us  [scatter_sum(): terms = total.astype(out_type if step == len(order) - 1 else terms.dtype)]
    concatenate x0 -> x25, local copies, waits for them, and re-layouts: none -> 26.5 us  [gather_all(): block = jnp.concatenate([first, second], axis=1)]
  transfers between devices with their start and end apart: 18 -> 96, of which waited for: 17 -> 42; matrix products, arithmetic and copies ran while one was open for 12% -> 32% of each run, Pallas kernels for 0% -> 0%
where the time goes in v1:
time: 940 us; the launch traced here: 929 us
  waiting for transfers between devices  314 us (33%)
  matrix products  192 us (20%)
  local copies, waits for them, and re-layouts  180 us (19%)
  other arithmetic  141 us (15%)
  starting transfers between devices  98.3 us (10%)
    ppermute x96, waiting for transfers between devices, swap(): return lax.ppermute(block, axes, pairs)  314 us
    ppermute x96, starting transfers between devices, swap(): return lax.ppermute(block, axes, pairs)  98.3 us
    unnamed x249, local copies, waits for them, and re-layouts  38 us
    dot_general x7, matrix products, tail_product(): lax.dot_general(left, right, (((1,), (1,)), ((), ())), preferred_element_...  35.2 us
    convert_element_type x32, other arithmetic, scatter_sum(): terms = total.astype(out_type if step == len(order) - 1 else terms.dtype)  29.2 us
    select_n x46, other arithmetic, gather_all(): first = jnp.where(mine == 0, own, other)  29.2 us
    dot_general x2, matrix products, score_terms(): jnp.einsum('qkgd,skd->kgqs', grad_heads, value_heads, preferred_element_t...  28.8 us
    dynamic_slice x4, local copies, waits for them, and re-layouts, scatter_sum(): keep = lax.dynamic_index_in_dim(split, mine, 1, keepdims=False)  28.5 us
  transfers between devices with their start and end apart: 96, of which 42 were waited for; matrix products, arithmetic and copies ran while one was open for 32% of the time, Pallas kernels for 0%

profile of v1, /device:TPU:0, one launch (start us, length us, event | category | flops | bytes accessed | tf_op | source)
XLA Modules:
  0.0 929.1 jit_solution(702966565267295844)
XLA Ops:
  54.3 9.2 collective-permute-done.20
  66.8 10.4 %collective-permute-done.14 = bf16[128,1024]{1,0:T(8,128)(2,1)S(1)} collective-permute-done((bf16[128,1024]{1,0:T(8,128)(2,1)S(1)}, bf16[128,1024]{1,0:T(8,128)(2,1)S(1)}, u32[]{:S(2)}, u32[]{:S(2)}) %collective-permute-start.14) | collective-permute-done | bytes 262176 | tf_op jit(solution)/shard_map/ppermute | solution.py:94
  86.4 13.2 %collective-permute-done.21 = bf16[128,2048]{1,0:T(8,128)(2,1)S(1)} collective-permute-done((bf16[128,2048]{1,0:T(8,128)(2,1)S(1)}, bf16[128,2048]{1,0:T(8,128)(2,1)S(1)}, u32[]{:S(2)}, u32[]{:S(2)}) %collective-permute-start.21) | collective-permute-done | bytes 524320 | tf_op jit(solution)/shard_map/ppermute | solution.py:94
  103.5 15.7 %collective-permute-done.15 = bf16[256,1024]{1,0:T(8,128)(2,1)S(1)} collective-permute-done((bf16[256,1024]{1,0:T(8,128)(2,1)S(1)}, bf16[256,1024]{1,0:T(8,128)(2,1)S(1)}, u32[]{:S(2)}, u32[]{:S(2)}) %collective-permute-start.15) | collective-permute-done | bytes 524320 | tf_op jit(solution)/shard_map/ppermute | solution.py:94
  121.1 12.2 %collective-permute-done.35 = bf16[128,3072]{1,0:T(8,128)(2,1)S(1)} collective-permute-done((bf16[128,3072]{1,0:T(8,128)(2,1)S(1)}, bf16[128,3072]{1,0:T(8,128)(2,1)S(1)}, u32[]{:S(2)}, u32[]{:S(2)}) %collective-permute-start.35) | collective-permute-done | bytes 786464 | tf_op jit(solution)/shard_map/ppermute | solution.py:94
  165.9 23.2 %collective-permute-done.10 = bf16[256,1024]{1,0:T(8,128)(2,1)} collective-permute-done((bf16[256,1024]{1,0:T(8,128)(2,1)}, bf16[256,1024]{1,0:T(8,128)(2,1)}, u32[]{:S(2)}, u32[]{:S(2)}) %collective-permute-start.10) | collective-permute-done | bytes 524320 | tf_op jit(solution)/shard_map/ppermute | solution.py:94
  190.7 9.5 %collective-permute-done.26 = bf16[256,1024]{1,0:T(8,128)(2,1)S(1)} collective-permute-done((bf16[256,1024]{1,0:T(8,128)(2,1)}, bf16[256,1024]{1,0:T(8,128)(2,1)S(1)}, u32[]{:S(2)}, u32[]{:S(2)}) %collective-permute-start.26) | collective-permute-done | bytes 524320 | tf_op jit(solution)/shard_map/ppermute | solution.py:94
  200.2 8.5 collective-permute-done.17
  282.2 8.1 fusion.6
  290.4 8.7 fusion.79
  299.1 7.4 fusion.126
  306.6 8.0 fusion.7
  370.2 11.4 %fusion.24 = (bf16[512,3072]{1,0:T(8,128)(2,1)}, bf16[512,3072]{1,0:T(8,128)(2,1)}, bf16[512,3072]{1,0:T(8,128)(2,1)}) fusion(f32[512,3072]{1,0:T(8,128)} %fusion.128, f32[512,3072]{1,0:T(8,128)} %fusion.129, bf16[3072,1024]{1,0:T(8,128)(2,1)S(1)} %bitcast.765, bf16[512,1024]{1,0:T(8,128)(2,1)S(1)} %bitcast.833), kind=kOutput, calls=%fused_computation.42 | convolution fusion | flops 3244818432 | bytes 29360128 | tf_op jit(solution)/shard_map/dot_general | solution.py:77
  426.5 10.2 %fusion.68 = bf16[1024,8,128]{0,2,1:T(8,128)(2,1)} fusion(bf16[256,8,2,128]{0,3,2,1:T(8,128)(2,1)S(1)} %bitcast.734, f32[8,2,256,1024]{2,3,1,0:T(8,128)} %get-tuple-element.182, f32[8,2,256]{2,1,0:T(2,128)} %bitcast.876), kind=kOutput, calls=%fused_computation.173 | convolution fusion | flops 1083179008 | bytes 19939328 | tf_op jit(solution)/shard_map/kgqs,qkgd->skd/dot_general | solution.py:308
  436.8 14.6 %fusion.3 = (f32[8,2,256]{2,1,0:T(2,128)}, f32[8,1024,256,2]{2,1,3,0:T(8,128)}) fusion(f32[8,2,256,1024]{2,3,1,0:T(8,128)} %get-tuple-element.182, f32[8,2,256]{2,1,0:T(2,128)} %bitcast.877, bf16[256,8,2,128]{0,3,2,1:T(8,128)(2,1)S(1)} %bitcast.735, bf16[1024,8,128,1]{2,1,0,3:T(8,128)(2,1)} %bitcast.738), kind=kOutput, calls=%fused_computation.7 | convolution fusion | flops 1086320640 | bytes 36732928 | tf_op jit(solution)/shard_map/qkgd,skd->kgqs/dot_general | solution.py:289
  451.4 7.7 fusion.5
  464.9 7.7 fusion.66
  473.2 10.2 %fusion.71 = bf16[1024,8,128]{0,2,1:T(8,128)(2,1)} fusion(bf16[256,8,2,128]{0,3,2,1:T(8,128)(2,1)S(1)} %bitcast.736, f32[8,2,256,1024]{2,3,1,0:T(8,128)} %get-tuple-element.180, f32[8,2,256]{2,1,0:T(2,128)} %bitcast.873), kind=kOutput, calls=%fused_computation.174 | convolution fusion | flops 1083179008 | bytes 19939328 | tf_op jit(solution)/shard_map/kgqs,qkgd->skd/dot_general | solution.py:308
  483.4 14.2 %fusion = (f32[8,2,256]{2,1,0:T(2,128)}, f32[8,1024,256,2]{2,1,3,0:T(8,128)}) fusion(f32[8,2,256,1024]{2,3,1,0:T(8,128)} %get-tuple-element.180, f32[8,2,256]{2,1,0:T(2,128)} %bitcast.874, bf16[256,8,2,128]{0,3,2,1:T(8,128)(2,1)S(1)} %bitcast.737, bf16[1024,8,128,1]{2,1,0,3:T(8,128)(2,1)} %bitcast.741), kind=kOutput, calls=%fused_computation.2 | convolution fusion | flops 1086320640 | bytes 36732928 | tf_op jit(solution)/shard_map/qkgd,skd->kgqs/dot_general | solution.py:289
  497.6 7.7 fusion.2
  511.2 7.5 fusion.67
  526.8 8.5 constant_dynamic-slice_fusion.24
  557.7 7.9 constant_dynamic-slice_fusion.30
  637.1 8.8 collective-permute-done.49
  646.7 10.4 %collective-permute-done.51 = bf16[1,256,1024]{1,2,0:T(8,128)(2,1)S(1)} collective-permute-done((bf16[1,256,1024]{1,2,0:T(8,128)(2,1)S(1)}, bf16[1,256,1024]{1,2,0:T(8,128)(2,1)S(1)}, u32[]{:S(2)}, u32[]{:S(2)}) %collective-permute-start.51) | collective-permute-done | bytes 524320 | tf_op jit(solution)/shard_map/ppermute | solution.py:94
  669.8 9.4 %collective-permute-done.55 = bf16[1,256,1024]{2,1,0:T(8,128)(2,1)} collective-permute-done((bf16[1,256,1024]{2,1,0:T(8,128)(2,1)}, bf16[1,256,1024]{2,1,0:T(8,128)(2,1)}, u32[]{:S(2)}, u32[]{:S(2)}) %collective-permute-start.55) | collective-permute-done | bytes 524320 | tf_op jit(solution)/shard_map/ppermute | solution.py:94
  720.2 28.7 %collective-permute-done.72 = bf16[8,32,1024]{2,1,0:T(8,128)(2,1)S(1)} collective-permute-done((bf16[8,32,1024]{2,1,0:T(8,128)(2,1)S(1)}, bf16[8,32,1024]{2,1,0:T(8,128)(2,1)S(1)}, u32[]{:S(2)}, u32[]{:S(2)}) %collective-permute-start.72) | collective-permute-done | bytes 524320 | tf_op jit(solution)/shard_map/ppermute | solution.py:94
  784.9 16.8 %collective-permute-done.68 = bf16[1,128,1024]{2,1,0:T(8,128)(2,1)S(1)} collective-permute-done((bf16[1,128,1024]{2,1,0:T(8,128)(2,1)S(1)}, bf16[1,128,1024]{2,1,0:T(8,128)(2,1)S(1)}, u32[]{:S(2)}, u32[]{:S(2)}) %collective-permute-start.68) | collective-permute-done | bytes 262176 | tf_op jit(solution)/shard_map/ppermute | solution.py:94
  828.4 14.6 %collective-permute-done.63 = bf16[2,64,2048]{2,1,0:T(8,128)(2,1)S(1)} collective-permute-done((bf16[2,64,2048]{2,1,0:T(8,128)(2,1)S(1)}, bf16[2,64,2048]{2,1,0:T(8,128)(2,1)S(1)}, u32[]{:S(2)}, u32[]{:S(2)}) %collective-permute-start.63) | collective-permute-done | bytes 524320 | tf_op jit(solution)/shard_map/ppermute | solution.py:94
  848.9 8.5 collective-permute-done.64
  868.5 26.0 %collective-permute-done.88 = bf16[1,128,3072]{2,1,0:T(8,128)(2,1)S(1)} collective-permute-done((bf16[1,128,3072]{2,1,0:T(8,128)(2,1)S(1)}, bf16[1,128,3072]{2,1,0:T(8,128)(2,1)S(1)}, u32[]{:S(2)}, u32[]{:S(2)}) %collective-permute-start.88) | collective-permute-done | bytes 786464 | tf_op jit(solution)/shard_map/ppermute | solution.py:94
  906.7 8.3 collective-permute-done.84
  (743 shorter events, 552.0 us)
Async XLA Ops:
  48.5 34.1 %collective-permute-start.39 = (bf16[64,3072]{1,0:T(8,128)(2,1)S(1)}, bf16[64,3072]{1,0:T(8,128)(2,1)S(1)}, u32[]{:S(2)}, u32[]{:S(2)}) collective-permute-start(bf16[64,3072]{1,0:T(8,128)(2,1)S(1)} %bitcast.870), channel_id=1, source_target_pairs={{0,2},{1,3},{2,0},{3,1},{4,6},{5,7},{6,4},{7,5},{8,10},{9,11},{10,... | collective-permute-start | bytes 1179656 | tf_op jit(solution)/shard_map/ppermute | solution.py:94
  51.2 32.8 %collective-permute-start.44 = (bf16[192,1024]{1,0:T(8,128)(2,1)S(1)}, bf16[192,1024]{1,0:T(8,128)(2,1)S(1)}, u32[]{:S(2)}, u32[]{:S(2)}) collective-permute-start(bf16[192,1024]{1,0:T(8,128)(2,1)S(1)} %bitcast.869), channel_id=1, source_target_pairs={{0,8},{1,9},{2,10},{3,11},{4,12},{5,13},{6,14},{7,15},{8,0},{9,1},... | collective-permute-start | bytes 1179656 | tf_op jit(solution)/shard_map/ppermute | solution.py:94
  63.7 35.8 %collective-permute-start.21 = (bf16[128,2048]{1,0:T(8,128)(2,1)S(1)}, bf16[128,2048]{1,0:T(8,128)(2,1)S(1)}, u32[]{:S(2)}, u32[]{:S(2)}) collective-permute-start(bf16[128,2048]{1,0:T(8,128)(2,1)S(1)} %bitcast.868), channel_id=1, source_target_pairs={{0,8},{1,9},{2,10},{3,11},{4,12},{5,13},{6,14},{7,15},{8,0},{9,1},... | collective-permute-start | bytes 1572872 | tf_op jit(solution)/shard_map/ppermute | solution.py:94
  82.5 36.7 %collective-permute-start.15 = (bf16[256,1024]{1,0:T(8,128)(2,1)S(1)}, bf16[256,1024]{1,0:T(8,128)(2,1)S(1)}, u32[]{:S(2)}, u32[]{:S(2)}) collective-permute-start(bf16[256,1024]{1,0:T(8,128)(2,1)S(1)} %bitcast.867), channel_id=1, source_target_pairs={{0,8},{1,9},{2,10},{3,11},{4,12},{5,13},{6,14},{7,15},{8,0},{9,1},... | collective-permute-start | bytes 1572872 | tf_op jit(solution)/shard_map/ppermute | solution.py:94
  82.6 36.8 %collective-permute-start.8 = (bf16[256,1024]{1,0:T(8,128)(2,1)S(1)}, bf16[256,1024]{1,0:T(8,128)(2,1)S(1)}, u32[]{:S(2)}, u32[]{:S(2)}) collective-permute-start(bf16[256,1024]{1,0:T(8,128)(2,1)S(1)} %bitcast.814), channel_id=1, source_target_pairs={{0,2},{1,3},{2,0},{3,1},{4,6},{5,7},{6,4},{7,5},{8,10},{9,11},{10,... | collective-permute-start | bytes 1572872 | tf_op jit(solution)/shard_map/ppermute | solution.py:94
  84.1 49.2 %collective-permute-start.35 = (bf16[128,3072]{1,0:T(8,128)(2,1)S(1)}, bf16[128,3072]{1,0:T(8,128)(2,1)S(1)}, u32[]{:S(2)}, u32[]{:S(2)}) collective-permute-start(bf16[128,3072]{1,0:T(8,128)(2,1)S(1)} %bitcast.860), channel_id=1, source_target_pairs={{0,8},{1,9},{2,10},{3,11},{4,12},{5,13},{6,14},{7,15},{8,0},{9,1},... | collective-permute-start | bytes 2359304 | tf_op jit(solution)/shard_map/ppermute | solution.py:94
  99.5 34.7 %collective-permute-start.45 = (bf16[384,1024]{1,0:T(8,128)(2,1)S(1)}, bf16[384,1024]{1,0:T(8,128)(2,1)S(1)}, u32[]{:S(2)}, u32[]{:S(2)}) collective-permute-start(bf16[384,1024]{1,0:T(8,128)(2,1)S(1)} %bitcast.811), channel_id=1, source_target_pairs={{0,4},{1,5},{2,6},{3,7},{4,0},{5,1},{6,2},{7,3},{8,12},{9,13},{10,... | collective-permute-start | bytes 2359304 | tf_op jit(solution)/shard_map/ppermute | solution.py:94
  99.7 33.8 %collective-permute-start.40 = (bf16[128,3072]{1,0:T(8,128)(2,1)S(1)}, bf16[128,3072]{1,0:T(8,128)(2,1)S(1)}, u32[]{:S(2)}, u32[]{:S(2)}) collective-permute-start(bf16[128,3072]{1,0:T(8,128)(2,1)S(1)} %bitcast.812), channel_id=1, source_target_pairs={{0,16},{1,17},{2,18},{3,19},{4,20},{5,21},{6,22},{7,23},{8,24},{9,... | collective-permute-start | bytes 2359304 | tf_op jit(solution)/shard_map/ppermute | solution.py:94
  137.2 73.1 %collective-permute-start.41 = (bf16[256,3072]{1,0:T(8,128)(2,1)}, bf16[256,3072]{1,0:T(8,128)(2,1)}, u32[]{:S(2)}, u32[]{:S(2)}) collective-permute-start(bf16[256,3072]{1,0:T(8,128)(2,1)} %bitcast.149), channel_id=1, source_target_pairs={{0,8},{1,9},{2,10},{3,11},{4,12},{5,13},{6,14},{7,15},{8,0},{9,1},... | collective-permute-start | bytes 4718600 | tf_op jit(solution)/shard_map/ppermute | solution.py:94
  140.2 80.5 %collective-permute-start.46 = (bf16[768,1024]{1,0:T(8,128)(2,1)}, bf16[768,1024]{1,0:T(8,128)(2,1)}, u32[]{:S(2)}, u32[]{:S(2)}) collective-permute-start(bf16[768,1024]{1,0:T(8,128)(2,1)} %bitcast.164), channel_id=1, source_target_pairs={{0,2},{1,3},{2,0},{3,1},{4,6},{5,7},{6,4},{7,5},{8,10},{9,11},{10,... | collective-permute-start | bytes 4718600 | tf_op jit(solution)/shard_map/ppermute | solution.py:94
  147.1 42.0 %collective-permute-start.10 = (bf16[256,1024]{1,0:T(8,128)(2,1)}, bf16[256,1024]{1,0:T(8,128)(2,1)}, u32[]{:S(2)}, u32[]{:S(2)}) collective-permute-start(bf16[256,1024]{1,0:T(8,128)(2,1)} %slice.141), channel_id=1, source_target_pairs={{0,2},{1,3},{2,0},{3,1},{4,6},{5,7},{6,4},{7,5},{8,10},{9,11},{10,... | collective-permute-start | bytes 1572872 | tf_op jit(solution)/shard_map/ppermute | solution.py:94
  162.2 38.0 %collective-permute-start.26 = (bf16[256,1024]{1,0:T(8,128)(2,1)}, bf16[256,1024]{1,0:T(8,128)(2,1)S(1)}, u32[]{:S(2)}, u32[]{:S(2)}) collective-permute-start(bf16[256,1024]{1,0:T(8,128)(2,1)} %copy.456), channel_id=1, source_target_pairs={{0,2},{1,3},{2,0},{3,1},{4,6},{5,7},{6,4},{7,5},{8,10},{9,11},{10,... | collective-permute-start | bytes 1572872 | tf_op jit(solution)/shard_map/ppermute | solution.py:94
  162.6 46.1 %collective-permute-start.17 = (bf16[256,1024]{1,0:T(8,128)(2,1)}, bf16[256,1024]{1,0:T(8,128)(2,1)S(1)}, u32[]{:S(2)}, u32[]{:S(2)}) collective-permute-start(bf16[256,1024]{1,0:T(8,128)(2,1)} %copy.451), channel_id=1, source_target_pairs={{0,2},{1,3},{2,0},{3,1},{4,6},{5,7},{6,4},{7,5},{8,10},{9,11},{10,... | collective-permute-start | bytes 1572872 | tf_op jit(solution)/shard_map/ppermute | solution.py:94
  200.2 48.5 %collective-permute-start.23 = (bf16[512,2048]{1,0:T(8,128)(2,1)}, bf16[512,2048]{1,0:T(8,128)(2,1)}, u32[]{:S(2)}, u32[]{:S(2)}) collective-permute-start(bf16[512,2048]{1,0:T(8,128)(2,1)} %bitcast.81), channel_id=1, source_target_pairs={{0,1},{1,0},{2,3},{3,2},{4,5},{5,4},{6,7},{7,6},{8,9},{9,8},{10,11... | collective-permute-start | bytes 6291464 | tf_op jit(solution)/shard_map/ppermute | solution.py:94
  208.7 45.9 %collective-permute-start.32 = (bf16[1024,1024]{1,0:T(8,128)(2,1)}, bf16[1024,1024]{1,0:T(8,128)(2,1)}, u32[]{:S(2)}, u32[]{:S(2)}) collective-permute-start(bf16[1024,1024]{1,0:T(8,128)(2,1)} %bitcast.122), channel_id=1, source_target_pairs={{0,1},{1,0},{2,3},{3,2},{4,5},{5,4},{6,7},{7,6},{8,9},{9,8},{10,11... | collective-permute-start | bytes 6291464 | tf_op jit(solution)/shard_map/ppermute | solution.py:94
  230.7 112.3 %collective-permute-start.37 = (bf16[512,3072]{1,0:T(8,128)(2,1)}, bf16[512,3072]{1,0:T(8,128)(2,1)}, u32[]{:S(2)}, u32[]{:S(2)}) collective-permute-start(bf16[512,3072]{1,0:T(8,128)(2,1)} %bitcast.137), channel_id=1, source_target_pairs={{0,1},{1,0},{2,3},{3,2},{4,5},{5,4},{6,7},{7,6},{8,9},{9,8},{10,11... | collective-permute-start | bytes 9437192 | tf_op jit(solution)/shard_map/ppermute | solution.py:94
  233.6 101.9 %collective-permute-start.47 = (bf16[1536,1024]{1,0:T(8,128)(2,1)}, bf16[1536,1024]{1,0:T(8,128)(2,1)}, u32[]{:S(2)}, u32[]{:S(2)}) collective-permute-start(bf16[1536,1024]{1,0:T(8,128)(2,1)} %bitcast.167), channel_id=1, source_target_pairs={{0,1},{1,0},{2,3},{3,2},{4,5},{5,4},{6,7},{7,6},{8,9},{9,8},{10,11... | collective-permute-start | bytes 9437192 | tf_op jit(solution)/shard_map/ppermute | solution.py:94
  239.4 103.6 %collective-permute-start.42 = (bf16[512,3072]{1,0:T(8,128)(2,1)}, bf16[512,3072]{1,0:T(8,128)(2,1)}, u32[]{:S(2)}, u32[]{:S(2)}) collective-permute-start(bf16[512,3072]{1,0:T(8,128)(2,1)} %bitcast.732), channel_id=1, source_target_pairs={{0,1},{1,0},{2,3},{3,2},{4,5},{5,4},{6,7},{7,6},{8,9},{9,8},{10,11... | collective-permute-start | bytes 9437192 | tf_op jit(solution)/shard_map/ppermute | solution.py:94
  248.7 67.2 %collective-permute-start.25 = (bf16[512,1024]{1,0:T(8,128)(2,1)}, bf16[512,1024]{1,0:T(8,128)(2,1)}, u32[]{:S(2)}, u32[]{:S(2)}) collective-permute-start(bf16[512,1024]{1,0:T(8,128)(2,1)} %bitcast.846), channel_id=1, source_target_pairs={{0,1},{1,0},{2,3},{3,2},{4,5},{5,4},{6,7},{7,6},{8,9},{9,8},{10,11... | collective-permute-start | bytes 3145736 | tf_op jit(solution)/shard_map/ppermute | solution.py:94
  545.7 85.4 %collective-permute-start.52 = (bf16[2,256,1024]{2,1,0:T(8,128)(2,1)}, bf16[2,256,1024]{2,1,0:T(8,128)(2,1)}, u32[]{:S(2)}, u32[]{:S(2)}) collective-permute-start(bf16[2,256,1024]{2,1,0:T(8,128)(2,1)} %bitcast.835), channel_id=1, source_target_pairs={{0,1},{1,0},{2,3},{3,2},{4,5},{5,4},{6,7},{7,6},{8,9},{9,8},{10,11... | collective-permute-start | bytes 3145736 | tf_op jit(solution)/shard_map/ppermute | solution.py:94
  548.8 160.4 %collective-permute-start.76 = (bf16[16,64,1024]{2,1,0:T(8,128)(2,1)}, bf16[16,64,1024]{2,1,0:T(8,128)(2,1)}, u32[]{:S(2)}, u32[]{:S(2)}) collective-permute-start(bf16[16,64,1024]{2,1,0:T(8,128)(2,1)} %dynamic-slice_bitcast_fusion.3), channel_id=1, source_target_pairs={{0,1},{1,0},{2,3},{3,2},{4,5},{5,4},{6,7},{7,6},{8,9},{9,8},{10,11... | collective-permute-start | bytes 6291464 | tf_op jit(solution)/shard_map/ppermute | solution.py:94
  566.8 60.3 %collective-permute-start.48 = (bf16[2,256,1024]{1,2,0:T(8,128)(2,1)}, bf16[2,256,1024]{1,2,0:T(8,128)(2,1)}, u32[]{:S(2)}, u32[]{:S(2)}) collective-permute-start(bf16[2,256,1024]{1,2,0:T(8,128)(2,1)} %bitcast.708), channel_id=1, source_target_pairs={{0,1},{1,0},{2,3},{3,2},{4,5},{5,4},{6,7},{7,6},{8,9},{9,8},{10,11... | collective-permute-start | bytes 3145736 | tf_op jit(solution)/shard_map/ppermute | solution.py:94
  627.2 126.0 %collective-permute-start.86 = (bf16[16,32,3072]{2,1,0:T(8,128)(2,1)}, bf16[16,32,3072]{2,1,0:T(8,128)(2,1)}, u32[]{:S(2)}, u32[]{:S(2)}) collective-permute-start(bf16[16,32,3072]{2,1,0:T(8,128)(2,1)} %dynamic-slice_bitcast_fusion.1), channel_id=1, source_target_pairs={{0,1},{1,0},{2,3},{3,2},{4,5},{5,4},{6,7},{7,6},{8,9},{9,8},{10,11... | collective-permute-start | bytes 9437192 | tf_op jit(solution)/shard_map/ppermute | solution.py:94
  629.3 128.9 %collective-permute-start.81 = (bf16[16,32,3072]{2,1,0:T(8,128)(2,1)}, bf16[16,32,3072]{2,1,0:T(8,128)(2,1)}, u32[]{:S(2)}, u32[]{:S(2)}) collective-permute-start(bf16[16,32,3072]{2,1,0:T(8,128)(2,1)} %dynamic-slice_bitcast_fusion.2), channel_id=1, source_target_pairs={{0,1},{1,0},{2,3},{3,2},{4,5},{5,4},{6,7},{7,6},{8,9},{9,8},{10,11... | collective-permute-start | bytes 9437192 | tf_op jit(solution)/shard_map/ppermute | solution.py:94
  668.5 44.0 %collective-permute-start.61 = (bf16[16,32,2048]{2,1,0:T(8,128)(2,1)}, bf16[16,32,2048]{2,1,0:T(8,128)(2,1)}, u32[]{:S(2)}, u32[]{:S(2)}) collective-permute-start(bf16[16,32,2048]{2,1,0:T(8,128)(2,1)} %dynamic-slice_bitcast_fusion.4), channel_id=1, source_target_pairs={{0,1},{1,0},{2,3},{3,2},{4,5},{5,4},{6,7},{7,6},{8,9},{9,8},{10,11... | collective-permute-start | bytes 6291464 | tf_op jit(solution)/shard_map/ppermute | solution.py:94
  712.5 39.1 %collective-permute-start.77 = (bf16[8,64,1024]{2,1,0:T(8,128)(2,1)S(1)}, bf16[8,64,1024]{2,1,0:T(8,128)(2,1)S(1)}, u32[]{:S(2)}, u32[]{:S(2)}) collective-permute-start(bf16[8,64,1024]{2,1,0:T(8,128)(2,1)S(1)} %dynamic-slice_bitcast_fusion.8), channel_id=1, source_target_pairs={{0,2},{1,3},{2,0},{3,1},{4,6},{5,7},{6,4},{7,5},{8,10},{9,11},{10,... | collective-permute-start | bytes 3145736 | tf_op jit(solution)/shard_map/ppermute | solution.py:94
  716.2 32.7 %collective-permute-start.72 = (bf16[8,32,1024]{2,1,0:T(8,128)(2,1)S(1)}, bf16[8,32,1024]{2,1,0:T(8,128)(2,1)S(1)}, u32[]{:S(2)}, u32[]{:S(2)}) collective-permute-start(bf16[8,32,1024]{2,1,0:T(8,128)(2,1)S(1)} %dynamic-slice_bitcast_fusion.15), channel_id=1, source_target_pairs={{0,2},{1,3},{2,0},{3,1},{4,6},{5,7},{6,4},{7,5},{8,10},{9,11},{10,... | collective-permute-start | bytes 1572872 | tf_op jit(solution)/shard_map/ppermute | solution.py:94
  718.8 43.6 %collective-permute-start.91 = (bf16[16,96,1024]{2,1,0:T(8,128)(2,1)S(1)}, bf16[16,96,1024]{2,1,0:T(8,128)(2,1)}, u32[]{:S(2)}, u32[]{:S(2)}) collective-permute-start(bf16[16,96,1024]{2,1,0:T(8,128)(2,1)S(1)} %copy-done.60), channel_id=1, source_target_pairs={{0,1},{1,0},{2,3},{3,2},{4,5},{5,4},{6,7},{7,6},{8,9},{9,8},{10,11... | collective-permute-start | bytes 9437192 | tf_op jit(solution)/shard_map/ppermute | solution.py:94
  758.3 69.8 %collective-permute-start.78 = (bf16[4,64,1024]{2,1,0:T(8,128)(2,1)}, bf16[4,64,1024]{2,1,0:T(8,128)(2,1)S(1)}, u32[]{:S(2)}, u32[]{:S(2)}) collective-permute-start(bf16[4,64,1024]{2,1,0:T(8,128)(2,1)} %dynamic-slice_bitcast_fusion.14), channel_id=1, source_target_pairs={{0,4},{1,5},{2,6},{3,7},{4,0},{5,1},{6,2},{7,3},{8,12},{9,13},{10,... | collective-permute-start | bytes 1572872 | tf_op jit(solution)/shard_map/ppermute | solution.py:94
  762.4 100.8 %collective-permute-start.87 = (bf16[2,128,3072]{2,1,0:T(8,128)(2,1)S(1)}, bf16[2,128,3072]{2,1,0:T(8,128)(2,1)S(1)}, u32[]{:S(2)}, u32[]{:S(2)}) collective-permute-start(bf16[2,128,3072]{2,1,0:T(8,128)(2,1)S(1)} %dynamic-slice_bitcast_fusion.6), channel_id=1, source_target_pairs={{0,8},{1,9},{2,10},{3,11},{4,12},{5,13},{6,14},{7,15},{8,0},{9,1},... | collective-permute-start | bytes 4718600 | tf_op jit(solution)/shard_map/ppermute | solution.py:94
  767.5 96.5 %collective-permute-start.82 = (bf16[4,64,3072]{2,1,0:T(8,128)(2,1)S(1)}, bf16[4,64,3072]{2,1,0:T(8,128)(2,1)S(1)}, u32[]{:S(2)}, u32[]{:S(2)}) collective-permute-start(bf16[4,64,3072]{2,1,0:T(8,128)(2,1)S(1)} %dynamic-slice_bitcast_fusion.7), channel_id=1, source_target_pairs={{0,4},{1,5},{2,6},{3,7},{4,0},{5,1},{6,2},{7,3},{8,12},{9,13},{10,... | collective-permute-start | bytes 4718600 | tf_op jit(solution)/shard_map/ppermute | solution.py:94
  775.3 91.5 %collective-permute-start.92 = (bf16[8,96,1024]{2,1,0:T(8,128)(2,1)S(1)}, bf16[8,96,1024]{2,1,0:T(8,128)(2,1)S(1)}, u32[]{:S(2)}, u32[]{:S(2)}) collective-permute-start(bf16[8,96,1024]{2,1,0:T(8,128)(2,1)S(1)} %dynamic-slice_bitcast_fusion.5), channel_id=1, source_target_pairs={{0,2},{1,3},{2,0},{3,1},{4,6},{5,7},{6,4},{7,5},{8,10},{9,11},{10,... | collective-permute-start | bytes 4718600 | tf_op jit(solution)/shard_map/ppermute | solution.py:94
  (184 other events, 2969.1 us)

commit v2 on v1

--- a/solution.py
+++ b/solution.py
@@ -94,24 +94,29 @@
     return lax.ppermute(block, axes, pairs)
 
 
-def scatter_sum(terms, axes, order, lead=1, out_type=jnp.float32):
+def scatter_step(terms, axes, order, step, out_type):
     count = lax.axis_size(axes)
-    me = lax.axis_index(axes)
-    tail = (terms.shape[0] // (lead * count),) + terms.shape[1:]
-    left = sorted(order, reverse=True)
-    for step, bit in enumerate(order):
-        place = left.index(bit)
-        above = lead << place
-        below = 1 << (len(left) - place - 1)
-        left.remove(bit)
-        split = terms.reshape((above, 2, below * tail[0]) + tail[1:])
-        mine = (me >> bit) & 1
-        away = lax.dynamic_index_in_dim(split, 1 - mine, 1, keepdims=False)
-        keep = lax.dynamic_index_in_dim(split, mine, 1, keepdims=False)
-        got = swap(away, axes, count, bit)
-        total = keep.astype(jnp.float32) + got.astype(jnp.float32)
-        terms = total.astype(out_type if step == len(order) - 1 else terms.dtype)
-    return terms.reshape((lead * tail[0],) + tail[1:])
+    mine = (lax.axis_index(axes) >> order[step]) & 1
+    above = 1 << sorted(order[step:], reverse=True).index(order[step])
+    split = terms.reshape((above, 2, terms.shape[0] // (2 * above)) + terms.shape[1:])
+    away = lax.dynamic_index_in_dim(split, 1 - mine, 1, keepdims=False)
+    keep = lax.dynamic_index_in_dim(split, mine, 1, keepdims=False)
+    got = swap(away, axes, count, order[step])
+    total = (keep.astype(jnp.float32) + got.astype(jnp.float32)).astype(out_type)
+    return total.reshape((terms.shape[0] // 2,) + terms.shape[1:])
+
+
+def scatter_sum(terms, axes, order, start=0):
+    for step in range(start, len(order)):
+        last = step == len(order) - 1
+        terms = scatter_step(terms, axes, order, step, jnp.float32 if last else terms.dtype)
+    return terms
+
+
+def step_all(terms, orders, step):
+    return [
+        scatter_step(term, AXES, order, step, term.dtype) for term, order in zip(terms, orders)
+    ]
 
 
 def gather_all(shard, axes, order, lead=1):
@@ -268,13 +273,22 @@
     up_grad = (hidden_grad * gate_silu).astype(jnp.bfloat16)
     w_gate_grad = lead_product(normed_two_low, gate_grad)
     w_up_grad = lead_product(normed_two_low, up_grad)
+    mlp_terms = [
+        grad.astype(jnp.bfloat16) for grad in (w_down_grad, w_gate_grad, w_up_grad)
+    ]
+    mlp_terms, gate_grad, up_grad = lax.optimization_barrier((mlp_terms, gate_grad, up_grad))
+    mlp_terms = step_all(mlp_terms, orders, 0)
     normed_two_grad = tail_product(gate_grad, gate_mat) + tail_product(up_grad, up_mat)
     resid_norm_grad, post_gain_grad = norm_backward(
         resid, inverse_two, gain_two.astype(jnp.float32), normed_two_grad
     )
     resid_grad = grad_low.astype(jnp.float32) + resid_norm_grad
     resid_low = resid_grad.astype(jnp.bfloat16)
-    w_out_grad = lead_product(attended_flat, resid_low)
+    mlp_terms, resid_low = lax.optimization_barrier((mlp_terms, resid_low))
+    mlp_terms = step_all(mlp_terms, orders, 1)
+    mlp_step = 2
+    out_terms = [lead_product(attended_flat, resid_low).astype(jnp.bfloat16)]
+    out_step = 0
     attended_grad = (
         tail_product(resid_low, out_mat)
         .astype(jnp.bfloat16)
@@ -314,20 +328,42 @@
             value_grad.reshape(seq_len, kv_width),
         )
 
-    backward = [
-        attend_back(
-            (
-                q_low[i],
-                key_all[i],
-                value_all[i],
-                q_segment[i],
-                k_segment[i],
-                log_totals[i],
-                attended_grad[i],
+    last_step = len(orders[0]) - 1
+    backward = []
+    for i in range(seq_count):
+        grad_seq = attended_grad[i]
+        if i > 0:
+            mlp_terms, out_terms, grad_seq, backward[-1] = lax.optimization_barrier(
+                (mlp_terms, out_terms, grad_seq, backward[-1])
             )
-        )
-        for i in range(seq_count)
-    ]
+            if mlp_step < last_step:
+                mlp_terms = step_all(mlp_terms, orders, mlp_step)
+                mlp_step += 1
+            if out_step < last_step:
+                out_terms = step_all(out_terms, orders[:1], out_step)
+                out_step += 1
+        backward.append(
+            attend_back(
+                (
+                    q_low[i],
+                    key_all[i],
+                    value_all[i],
+                    q_segment[i],
+                    k_segment[i],
+                    log_totals[i],
+                    grad_seq,
+                )
+            )
+        )
+    mlp_terms, out_terms, backward[-1] = lax.optimization_barrier(
+        (mlp_terms, out_terms, backward[-1])
+    )
+    if mlp_step < last_step:
+        mlp_terms = step_all(mlp_terms, orders, mlp_step)
+        mlp_step += 1
+    if out_step < last_step:
+        out_terms = step_all(out_terms, orders[:1], out_step)
+        out_step += 1
     q_rot_grad = jnp.stack([item[0] for item in backward])
     key_part, value_part = [
         jnp.stack(
@@ -349,6 +385,9 @@
         unrotate(k_rot_grad, cosine_table, sine_table),
     )
     queries_grad = q_pre_grad.astype(jnp.bfloat16).reshape(row_count, q_heads * head_dim)
+    mlp_terms, out_terms, queries_grad = lax.optimization_barrier(
+        (mlp_terms, out_terms, queries_grad)
+    )
     keys_grad = k_pre_grad.astype(jnp.bfloat16).reshape(row_count, kv_width)
     values_low_grad = value_part.astype(jnp.bfloat16).reshape(row_count, kv_width)
     w_query_grad = lead_product(normed_low, queries_grad)
@@ -384,11 +423,11 @@
         scatter_sum(w_value_grad.astype(jnp.bfloat16), AXES, orders[0]),
         q_gain_sum,
         k_gain_sum,
-        scatter_sum(w_out_grad.astype(jnp.bfloat16), AXES, orders[0]),
+        scatter_sum(out_terms[0], AXES, orders[0], out_step),
         post_gain_sum,
-        scatter_sum(w_gate_grad.astype(jnp.bfloat16), AXES, orders[1]),
-        scatter_sum(w_up_grad.astype(jnp.bfloat16), AXES, orders[2]),
-        scatter_sum(w_down_grad.astype(jnp.bfloat16), AXES, orders[0]),
+        scatter_sum(mlp_terms[1], AXES, orders[1], mlp_step),
+        scatter_sum(mlp_terms[2], AXES, orders[2], mlp_step),
+        scatter_sum(mlp_terms[0], AXES, orders[0], mlp_step),
     )
 
 

time: 940 us -> 824 us (0.88)
  waiting for transfers between devices: 314 us -> 226 us
  local copies, waits for them, and re-layouts: 180 us -> 135 us
  other arithmetic: 141 us -> 160 us
    ppermute x96, waiting for transfers between devices: 314 us -> 226 us  [swap(): return lax.ppermute(block, axes, pairs)]
    dynamic_slice x11 -> x3, local copies, waits for them, and re-layouts: 41.1 us -> 0.05 us  [scatter_step(): away = lax.dynamic_index_in_dim(split, 1 - mine, 1, keepdims=False)]
    convert_element_type x4 -> x0, local copies, waits for them, and re-layouts: 17 us -> none  [local(): item[j].astype(jnp.bfloat16)]
    convert_element_type x32 -> x31, other arithmetic: 29.2 us -> 45.9 us  [the longest x30 42.3 us: scatter_step(): (keep.astype(jnp.float32) + got.astype(jnp.float32)).astype(out_type)]
    optimization_barrier x0 -> x4, local copies, waits for them, and re-layouts: none -> 13.4 us  [the longest x2 7.86 us: local(): lax.optimization_barrier((mlp_terms, out_terms, grad_seq, backward[-1]))]
    squeeze x41 -> x45, local copies, waits for them, and re-layouts: 23.3 us -> 34.1 us  [scatter_step(): away = lax.dynamic_index_in_dim(split, 1 - mine, 1, keepdims=False)]
    unnamed x249 -> x286, local copies, waits for them, and re-layouts: 38 us -> 33.2 us
  transfers between devices with their start and end apart: 96 -> 96, of which waited for: 42 -> 33; matrix products, arithmetic and copies ran while one was open for 32% -> 39% of each run, Pallas kernels for 0% -> 0%
where the time goes in v2:
time: 824 us; the launch traced here: 814 us
  waiting for transfers between devices  226 us (27%)
  matrix products  191 us (23%)
  other arithmetic  160 us (19%)
  local copies, waits for them, and re-layouts  135 us (16%)
  starting transfers between devices  97.9 us (12%)
    ppermute x96, waiting for transfers between devices, swap(): return lax.ppermute(block, axes, pairs)  226 us
    ppermute x96, starting transfers between devices, swap(): return lax.ppermute(block, axes, pairs)  97.9 us
    convert_element_type x30, other arithmetic, scatter_step(): (keep.astype(jnp.float32) + got.astype(jnp.float32)).astype(out_type)  42.3 us
    squeeze x45, local copies, waits for them, and re-layouts, scatter_step(): away = lax.dynamic_index_in_dim(split, 1 - mine, 1, keepdims=False)  34.1 us
    unnamed x286, local copies, waits for them, and re-layouts  33.2 us
    dot_general x7, matrix products, tail_product(): lax.dot_general(left, right, (((1,), (1,)), ((), ())), preferred_element_...  30.1 us
    dot_general x7, matrix products, lead_product(): lax.dot_general(left, right, (((0,), (0,)), ((), ())), preferred_element_...  29.8 us
    select_n x46, other arithmetic, gather_all(): first = jnp.where(mine == 0, own, other)  29.4 us
  transfers between devices with their start and end apart: 96, of which 33 were waited for; matrix products, arithmetic and copies ran while one was open for 39% of the time, Pallas kernels for 0%

profile of v2, /device:TPU:0, one launch (start us, length us, event | category | flops | bytes accessed | tf_op | source)
XLA Modules:
  0.0 814.1 jit_solution(17988817474299039083)
XLA Ops:
  38.7 7.9 collective-permute-start.20
  54.9 9.2 %collective-permute-done.20 = bf16[64,2048]{1,0:T(8,128)(2,1)S(1)} collective-permute-done((bf16[64,2048]{1,0:T(8,128)(2,1)S(1)}, bf16[64,2048]{1,0:T(8,128)(2,1)S(1)}, u32[]{:S(2)}, u32[]{:S(2)}) %collective-permute-start.20) | collective-permute-done | bytes 262176 | tf_op jit(solution)/shard_map/ppermute | solution.py:94
  67.2 10.6 %collective-permute-done.14 = bf16[128,1024]{1,0:T(8,128)(2,1)S(1)} collective-permute-done((bf16[128,1024]{1,0:T(8,128)(2,1)S(1)}, bf16[128,1024]{1,0:T(8,128)(2,1)S(1)}, u32[]{:S(2)}, u32[]{:S(2)}) %collective-permute-start.14) | collective-permute-done | bytes 262176 | tf_op jit(solution)/shard_map/ppermute | solution.py:94
  87.0 13.1 %collective-permute-done.21 = bf16[128,2048]{1,0:T(8,128)(2,1)S(1)} collective-permute-done((bf16[128,2048]{1,0:T(8,128)(2,1)S(1)}, bf16[128,2048]{1,0:T(8,128)(2,1)S(1)}, u32[]{:S(2)}, u32[]{:S(2)}) %collective-permute-start.21) | collective-permute-done | bytes 524320 | tf_op jit(solution)/shard_map/ppermute | solution.py:94
  104.4 15.3 %collective-permute-done.15 = bf16[256,1024]{1,0:T(8,128)(2,1)S(1)} collective-permute-done((bf16[256,1024]{1,0:T(8,128)(2,1)S(1)}, bf16[256,1024]{1,0:T(8,128)(2,1)S(1)}, u32[]{:S(2)}, u32[]{:S(2)}) %collective-permute-start.15) | collective-permute-done | bytes 524320 | tf_op jit(solution)/shard_map/ppermute | solution.py:94
  121.1 12.3 %collective-permute-done.35 = bf16[128,3072]{1,0:T(8,128)(2,1)S(1)} collective-permute-done((bf16[128,3072]{1,0:T(8,128)(2,1)S(1)}, bf16[128,3072]{1,0:T(8,128)(2,1)S(1)}, u32[]{:S(2)}, u32[]{:S(2)}) %collective-permute-start.35) | collective-permute-done | bytes 786464 | tf_op jit(solution)/shard_map/ppermute | solution.py:94
  165.1 23.3 %collective-permute-done.10 = bf16[256,1024]{1,0:T(8,128)(2,1)} collective-permute-done((bf16[256,1024]{1,0:T(8,128)(2,1)}, bf16[256,1024]{1,0:T(8,128)(2,1)}, u32[]{:S(2)}, u32[]{:S(2)}) %collective-permute-start.10) | collective-permute-done | bytes 524320 | tf_op jit(solution)/shard_map/ppermute | solution.py:94
  189.8 9.7 %collective-permute-done.26 = bf16[256,1024]{1,0:T(8,128)(2,1)S(1)} collective-permute-done((bf16[256,1024]{1,0:T(8,128)(2,1)}, bf16[256,1024]{1,0:T(8,128)(2,1)S(1)}, u32[]{:S(2)}, u32[]{:S(2)}) %collective-permute-start.26) | collective-permute-done | bytes 524320 | tf_op jit(solution)/shard_map/ppermute | solution.py:94
  199.5 9.2 %collective-permute-done.17 = bf16[256,1024]{1,0:T(8,128)(2,1)S(1)} collective-permute-done((bf16[256,1024]{1,0:T(8,128)(2,1)}, bf16[256,1024]{1,0:T(8,128)(2,1)S(1)}, u32[]{:S(2)}, u32[]{:S(2)}) %collective-permute-start.17) | collective-permute-done | bytes 524320 | tf_op jit(solution)/shard_map/ppermute | solution.py:94
  212.8 7.8 collective-permute-done.36
  274.4 7.4 fusion.115
  281.8 8.2 %fusion.6 = f32[8,2,256]{2,1,0:T(2,128)S(1)} fusion(f32[8,2,256,1024]{2,3,1,0:T(8,128)} %get-tuple-element.235, f32[8,2,256]{2,1,0:T(2,128)S(1)} %get-tuple-element.234), kind=kLoop, calls=%fused_computation.18 | loop fusion | flops 8384512 | bytes 16809984 | tf_op jit(solution)/shard_map/reduce_sum | solution.py:240
  290.0 8.6 %fusion.63 = bf16[8,128,2,256]{3,1,2,0:T(8,128)(2,1)} fusion(f32[8,2,256,1024]{2,3,1,0:T(8,128)} %get-tuple-element.235, f32[8,2,256]{2,1,0:T(2,128)S(1)} %fusion.6, f32[8,2,256]{2,1,0:T(2,128)S(1)} %get-tuple-element.234, bf16[1024,8,128,1]{2,1,0,3:T(8,128)(2,1)S(1)} %bitcast.773), kind=kOutput, calls=%fused_computation.188 | convolution fusion | flops 1086849024 | bytes 19955712 | tf_op jit(solution)/shard_map/kgqs,skd->qkgd/dot_general | solution.py:242
  298.6 7.4 fusion.114
  306.0 8.0 fusion.7
  362.0 10.2 %fusion.24 = (bf16[512,3072]{1,0:T(8,128)(2,1)}, bf16[512,3072]{1,0:T(8,128)(2,1)}, bf16[512,3072]{1,0:T(8,128)(2,1)}) fusion(f32[512,3072]{1,0:T(8,128)} %fusion.116, f32[512,3072]{1,0:T(8,128)S(1)} %copy-done.116, bf16[3072,1024]{1,0:T(8,128)(2,1)S(1)} %bitcast.811, bf16[512,1024]{1,0:T(8,128)(2,1)S(1)} %bitcast.908), kind=kOutput, calls=%fused_computation.42 | convolution fusion | flops 3244818432 | bytes 29360128 | tf_op jit(solution)/shard_map/dot_general | solution.py:77
  372.1 7.4 convolution_convert_fusion
  411.8 8.7 %add_convert_fusion = bf16[512,1024]{1,0:T(8,128)(2,1)} fusion(f32[512,1024]{1,0:T(8,128)S(1)} %copy-done.36, bf16[512,3072]{1,0:T(8,128)(2,1)} %get-tuple-element.85, bf16[3072,1024]{1,0:T(8,128)(2,1)} %bitcast.808), kind=kOutput, calls=%fused_computation.150 | convolution fusion | flops 3222274048 | bytes 12582912 | tf_op jit(solution)/shard_map/dot_general | solution.py:264
  439.8 10.2 %fusion.12 = bf16[8,128,1024,1]{2,1,3,0:T(8,128)(2,1)} fusion(bf16[256,8,2,128]{0,3,2,1:T(8,128)(2,1)S(1)} %bitcast.768, f32[8,2,256,1024]{2,3,1,0:T(8,128)} %get-tuple-element.235, f32[8,2,256]{2,1,0:T(2,128)} %bitcast.926), kind=kOutput, calls=%fused_computation.23 | convolution fusion | flops 1082130432 | bytes 19939328 | tf_op jit(solution)/shard_map/kgqs,qkgd->skd/dot_general | solution.py:322
  450.0 14.2 %fusion.3 = (f32[8,2,256]{2,1,0:T(2,128)}, f32[8,1024,256,2]{2,1,3,0:T(8,128)}) fusion(f32[8,2,256,1024]{2,3,1,0:T(8,128)} %get-tuple-element.235, f32[8,2,256]{2,1,0:T(2,128)} %bitcast.927, bf16[256,8,2,128]{0,3,2,1:T(8,128)(2,1)S(1)} %bitcast.769, bf16[1024,8,128,1]{2,1,0,3:T(8,128)(2,1)} %bitcast.772), kind=kOutput, calls=%fused_computation.7 | convolution fusion | flops 1086320640 | bytes 36732928 | tf_op jit(solution)/shard_map/qkgd,skd->kgqs/dot_general | solution.py:303
  473.6 7.9 fusion.5
  487.3 7.7 bitcast_multiply_fusion.5
  499.4 8.4 %collective-permute-done.51 = bf16[8,96,1024]{2,1,0:T(8,128)(2,1)} collective-permute-done((bf16[8,96,1024]{2,1,0:T(8,128)(2,1)}, bf16[8,96,1024]{2,1,0:T(8,128)(2,1)}, u32[]{:S(2)}, u32[]{:S(2)}) %collective-permute-start.51) | collective-permute-done | bytes 1572896 | tf_op jit(solution)/shard_map/ppermute | solution.py:94
  517.2 10.3 %fusion.10 = bf16[8,128,1024,1]{2,1,3,0:T(8,128)(2,1)} fusion(bf16[256,8,2,128]{0,3,2,1:T(8,128)(2,1)S(1)} %bitcast.770, f32[8,2,256,1024]{2,3,1,0:T(8,128)} %get-tuple-element.233, f32[8,2,256]{2,1,0:T(2,128)} %bitcast.923), kind=kOutput, calls=%fused_computation.22 | convolution fusion | flops 1082130432 | bytes 19939328 | tf_op jit(solution)/shard_map/kgqs,qkgd->skd/dot_general | solution.py:322
  527.5 14.2 %fusion = (f32[8,2,256]{2,1,0:T(2,128)}, f32[8,1024,256,2]{2,1,3,0:T(8,128)}) fusion(f32[8,2,256,1024]{2,3,1,0:T(8,128)} %get-tuple-element.233, f32[8,2,256]{2,1,0:T(2,128)} %bitcast.924, bf16[256,8,2,128]{0,3,2,1:T(8,128)(2,1)S(1)} %bitcast.771, bf16[1024,8,128,1]{2,1,0,3:T(8,128)(2,1)} %bitcast.775), kind=kOutput, calls=%fused_computation.2 | convolution fusion | flops 1086320640 | bytes 36732928 | tf_op jit(solution)/shard_map/qkgd,skd->kgqs/dot_general | solution.py:303
  541.7 8.1 fusion.2
  595.0 17.2 %collective-permute-done.56 = bf16[1,128,3072]{2,1,0:T(8,128)(2,1)} collective-permute-done((bf16[1,128,3072]{2,1,0:T(8,128)(2,1)}, bf16[1,128,3072]{2,1,0:T(8,128)(2,1)}, u32[]{:S(2)}, u32[]{:S(2)}) %collective-permute-start.56) | collective-permute-done | bytes 786464 | tf_op jit(solution)/shard_map/ppermute | solution.py:94
  740.8 7.5 collective-permute-done.81
  753.0 7.8 collective-permute-done.82
  762.4 16.4 %collective-permute-done.87 = bf16[4,32,1024]{2,1,0:T(8,128)(2,1)S(1)} collective-permute-done((bf16[4,32,1024]{2,1,0:T(8,128)(2,1)S(1)}, bf16[4,32,1024]{2,1,0:T(8,128)(2,1)S(1)}, u32[]{:S(2)}, u32[]{:S(2)}) %collective-permute-start.87) | collective-permute-done | bytes 262176 | tf_op jit(solution)/shard_map/ppermute | solution.py:94
  785.9 8.1 collective-permute-done.77
  797.9 10.0 %collective-permute-done.78 = bf16[1,64,2048]{2,1,0:T(8,128)(2,1)S(1)} collective-permute-done((bf16[1,64,2048]{2,1,0:T(8,128)(2,1)S(1)}, bf16[1,64,2048]{2,1,0:T(8,128)(2,1)S(1)}, u32[]{:S(2)}, u32[]{:S(2)}) %collective-permute-start.78) | collective-permute-done | bytes 262176 | tf_op jit(solution)/shard_map/ppermute | solution.py:94
  (777 shorter events, 478.1 us)
Async XLA Ops:
  49.1 34.1 %collective-permute-start.39 = (bf16[64,3072]{1,0:T(8,128)(2,1)S(1)}, bf16[64,3072]{1,0:T(8,128)(2,1)S(1)}, u32[]{:S(2)}, u32[]{:S(2)}) collective-permute-start(bf16[64,3072]{1,0:T(8,128)(2,1)S(1)} %bitcast.920), channel_id=1, source_target_pairs={{0,2},{1,3},{2,0},{3,1},{4,6},{5,7},{6,4},{7,5},{8,10},{9,11},{10,... | collective-permute-start | bytes 1179656 | tf_op jit(solution)/shard_map/ppermute | solution.py:94
  51.8 32.9 %collective-permute-start.44 = (bf16[192,1024]{1,0:T(8,128)(2,1)S(1)}, bf16[192,1024]{1,0:T(8,128)(2,1)S(1)}, u32[]{:S(2)}, u32[]{:S(2)}) collective-permute-start(bf16[192,1024]{1,0:T(8,128)(2,1)S(1)} %bitcast.919), channel_id=1, source_target_pairs={{0,8},{1,9},{2,10},{3,11},{4,12},{5,13},{6,14},{7,15},{8,0},{9,1},... | collective-permute-start | bytes 1179656 | tf_op jit(solution)/shard_map/ppermute | solution.py:94
  64.3 35.8 %collective-permute-start.21 = (bf16[128,2048]{1,0:T(8,128)(2,1)S(1)}, bf16[128,2048]{1,0:T(8,128)(2,1)S(1)}, u32[]{:S(2)}, u32[]{:S(2)}) collective-permute-start(bf16[128,2048]{1,0:T(8,128)(2,1)S(1)} %bitcast.918), channel_id=1, source_target_pairs={{0,8},{1,9},{2,10},{3,11},{4,12},{5,13},{6,14},{7,15},{8,0},{9,1},... | collective-permute-start | bytes 1572872 | tf_op jit(solution)/shard_map/ppermute | solution.py:94
  83.0 36.7 %collective-permute-start.15 = (bf16[256,1024]{1,0:T(8,128)(2,1)S(1)}, bf16[256,1024]{1,0:T(8,128)(2,1)S(1)}, u32[]{:S(2)}, u32[]{:S(2)}) collective-permute-start(bf16[256,1024]{1,0:T(8,128)(2,1)S(1)} %bitcast.917), channel_id=1, source_target_pairs={{0,8},{1,9},{2,10},{3,11},{4,12},{5,13},{6,14},{7,15},{8,0},{9,1},... | collective-permute-start | bytes 1572872 | tf_op jit(solution)/shard_map/ppermute | solution.py:94
  83.1 36.9 %collective-permute-start.8 = (bf16[256,1024]{1,0:T(8,128)(2,1)S(1)}, bf16[256,1024]{1,0:T(8,128)(2,1)S(1)}, u32[]{:S(2)}, u32[]{:S(2)}) collective-permute-start(bf16[256,1024]{1,0:T(8,128)(2,1)S(1)} %bitcast.860), channel_id=1, source_target_pairs={{0,2},{1,3},{2,0},{3,1},{4,6},{5,7},{6,4},{7,5},{8,10},{9,11},{10,... | collective-permute-start | bytes 1572872 | tf_op jit(solution)/shard_map/ppermute | solution.py:94
  84.7 48.6 %collective-permute-start.35 = (bf16[128,3072]{1,0:T(8,128)(2,1)S(1)}, bf16[128,3072]{1,0:T(8,128)(2,1)S(1)}, u32[]{:S(2)}, u32[]{:S(2)}) collective-permute-start(bf16[128,3072]{1,0:T(8,128)(2,1)S(1)} %bitcast.910), channel_id=1, source_target_pairs={{0,8},{1,9},{2,10},{3,11},{4,12},{5,13},{6,14},{7,15},{8,0},{9,1},... | collective-permute-start | bytes 2359304 | tf_op jit(solution)/shard_map/ppermute | solution.py:94
  100.1 34.1 %collective-permute-start.45 = (bf16[384,1024]{1,0:T(8,128)(2,1)S(1)}, bf16[384,1024]{1,0:T(8,128)(2,1)S(1)}, u32[]{:S(2)}, u32[]{:S(2)}) collective-permute-start(bf16[384,1024]{1,0:T(8,128)(2,1)S(1)} %bitcast.857), channel_id=1, source_target_pairs={{0,4},{1,5},{2,6},{3,7},{4,0},{5,1},{6,2},{7,3},{8,12},{9,13},{10,... | collective-permute-start | bytes 2359304 | tf_op jit(solution)/shard_map/ppermute | solution.py:94
  100.3 33.2 %collective-permute-start.40 = (bf16[128,3072]{1,0:T(8,128)(2,1)S(1)}, bf16[128,3072]{1,0:T(8,128)(2,1)S(1)}, u32[]{:S(2)}, u32[]{:S(2)}) collective-permute-start(bf16[128,3072]{1,0:T(8,128)(2,1)S(1)} %bitcast.858), channel_id=1, source_target_pairs={{0,16},{1,17},{2,18},{3,19},{4,20},{5,21},{6,22},{7,23},{8,24},{9,... | collective-permute-start | bytes 2359304 | tf_op jit(solution)/shard_map/ppermute | solution.py:94
  137.1 73.1 %collective-permute-start.41 = (bf16[256,3072]{1,0:T(8,128)(2,1)}, bf16[256,3072]{1,0:T(8,128)(2,1)}, u32[]{:S(2)}, u32[]{:S(2)}) collective-permute-start(bf16[256,3072]{1,0:T(8,128)(2,1)} %bitcast.149), channel_id=1, source_target_pairs={{0,8},{1,9},{2,10},{3,11},{4,12},{5,13},{6,14},{7,15},{8,0},{9,1},... | collective-permute-start | bytes 4718600 | tf_op jit(solution)/shard_map/ppermute | solution.py:94
  139.5 81.8 %collective-permute-start.46 = (bf16[768,1024]{1,0:T(8,128)(2,1)}, bf16[768,1024]{1,0:T(8,128)(2,1)}, u32[]{:S(2)}, u32[]{:S(2)}) collective-permute-start(bf16[768,1024]{1,0:T(8,128)(2,1)} %bitcast.164), channel_id=1, source_target_pairs={{0,2},{1,3},{2,0},{3,1},{4,6},{5,7},{6,4},{7,5},{8,10},{9,11},{10,... | collective-permute-start | bytes 4718600 | tf_op jit(solution)/shard_map/ppermute | solution.py:94
  146.2 42.2 %collective-permute-start.10 = (bf16[256,1024]{1,0:T(8,128)(2,1)}, bf16[256,1024]{1,0:T(8,128)(2,1)}, u32[]{:S(2)}, u32[]{:S(2)}) collective-permute-start(bf16[256,1024]{1,0:T(8,128)(2,1)} %slice.141), channel_id=1, source_target_pairs={{0,2},{1,3},{2,0},{3,1},{4,6},{5,7},{6,4},{7,5},{8,10},{9,11},{10,... | collective-permute-start | bytes 1572872 | tf_op jit(solution)/shard_map/ppermute | solution.py:94
  161.4 38.1 %collective-permute-start.26 = (bf16[256,1024]{1,0:T(8,128)(2,1)}, bf16[256,1024]{1,0:T(8,128)(2,1)S(1)}, u32[]{:S(2)}, u32[]{:S(2)}) collective-permute-start(bf16[256,1024]{1,0:T(8,128)(2,1)} %copy.439), channel_id=1, source_target_pairs={{0,2},{1,3},{2,0},{3,1},{4,6},{5,7},{6,4},{7,5},{8,10},{9,11},{10,... | collective-permute-start | bytes 1572872 | tf_op jit(solution)/shard_map/ppermute | solution.py:94
  161.7 47.0 %collective-permute-start.17 = (bf16[256,1024]{1,0:T(8,128)(2,1)}, bf16[256,1024]{1,0:T(8,128)(2,1)S(1)}, u32[]{:S(2)}, u32[]{:S(2)}) collective-permute-start(bf16[256,1024]{1,0:T(8,128)(2,1)} %copy.434), channel_id=1, source_target_pairs={{0,2},{1,3},{2,0},{3,1},{4,6},{5,7},{6,4},{7,5},{8,10},{9,11},{10,... | collective-permute-start | bytes 1572872 | tf_op jit(solution)/shard_map/ppermute | solution.py:94
  188.4 32.3 %collective-permute-start.36 = (bf16[256,3072]{1,0:T(8,128)(2,1)S(1)}, bf16[256,3072]{1,0:T(8,128)(2,1)S(1)}, u32[]{:S(2)}, u32[]{:S(2)}) collective-permute-start(bf16[256,3072]{1,0:T(8,128)(2,1)S(1)} %bitcast.830), channel_id=1, source_target_pairs={{0,4},{1,5},{2,6},{3,7},{4,0},{5,1},{6,2},{7,3},{8,12},{9,13},{10,... | collective-permute-start | bytes 4718600 | tf_op jit(solution)/shard_map/ppermute | solution.py:94
  199.5 47.1 %collective-permute-start.23 = (bf16[512,2048]{1,0:T(8,128)(2,1)}, bf16[512,2048]{1,0:T(8,128)(2,1)}, u32[]{:S(2)}, u32[]{:S(2)}) collective-permute-start(bf16[512,2048]{1,0:T(8,128)(2,1)} %bitcast.81), channel_id=1, source_target_pairs={{0,1},{1,0},{2,3},{3,2},{4,5},{5,4},{6,7},{7,6},{8,9},{9,8},{10,11... | collective-permute-start | bytes 6291464 | tf_op jit(solution)/shard_map/ppermute | solution.py:94
  208.7 43.9 %collective-permute-start.32 = (bf16[1024,1024]{1,0:T(8,128)(2,1)}, bf16[1024,1024]{1,0:T(8,128)(2,1)}, u32[]{:S(2)}, u32[]{:S(2)}) collective-permute-start(bf16[1024,1024]{1,0:T(8,128)(2,1)} %bitcast.122), channel_id=1, source_target_pairs={{0,1},{1,0},{2,3},{3,2},{4,5},{5,4},{6,7},{7,6},{8,9},{9,8},{10,11... | collective-permute-start | bytes 6291464 | tf_op jit(solution)/shard_map/ppermute | solution.py:94
  231.2 109.2 %collective-permute-start.37 = (bf16[512,3072]{1,0:T(8,128)(2,1)}, bf16[512,3072]{1,0:T(8,128)(2,1)}, u32[]{:S(2)}, u32[]{:S(2)}) collective-permute-start(bf16[512,3072]{1,0:T(8,128)(2,1)} %bitcast.137), channel_id=1, source_target_pairs={{0,1},{1,0},{2,3},{3,2},{4,5},{5,4},{6,7},{7,6},{8,9},{9,8},{10,11... | collective-permute-start | bytes 9437192 | tf_op jit(solution)/shard_map/ppermute | solution.py:94
  234.2 98.8 %collective-permute-start.47 = (bf16[1536,1024]{1,0:T(8,128)(2,1)}, bf16[1536,1024]{1,0:T(8,128)(2,1)}, u32[]{:S(2)}, u32[]{:S(2)}) collective-permute-start(bf16[1536,1024]{1,0:T(8,128)(2,1)} %bitcast.167), channel_id=1, source_target_pairs={{0,1},{1,0},{2,3},{3,2},{4,5},{5,4},{6,7},{7,6},{8,9},{9,8},{10,11... | collective-permute-start | bytes 9437192 | tf_op jit(solution)/shard_map/ppermute | solution.py:94
  238.4 102.1 %collective-permute-start.42 = (bf16[512,3072]{1,0:T(8,128)(2,1)}, bf16[512,3072]{1,0:T(8,128)(2,1)}, u32[]{:S(2)}, u32[]{:S(2)}) collective-permute-start(bf16[512,3072]{1,0:T(8,128)(2,1)} %bitcast.152), channel_id=1, source_target_pairs={{0,1},{1,0},{2,3},{3,2},{4,5},{5,4},{6,7},{7,6},{8,9},{9,8},{10,11... | collective-permute-start | bytes 9437192 | tf_op jit(solution)/shard_map/ppermute | solution.py:94
  246.6 68.7 %collective-permute-start.25 = (bf16[512,1024]{1,0:T(8,128)(2,1)}, bf16[512,1024]{1,0:T(8,128)(2,1)}, u32[]{:S(2)}, u32[]{:S(2)}) collective-permute-start(bf16[512,1024]{1,0:T(8,128)(2,1)} %bitcast.893), channel_id=1, source_target_pairs={{0,1},{1,0},{2,3},{3,2},{4,5},{5,4},{6,7},{7,6},{8,9},{9,8},{10,11... | collective-permute-start | bytes 3145736 | tf_op jit(solution)/shard_map/ppermute | solution.py:94
  467.0 44.0 %collective-permute-start.53 = (bf16[2,128,3072]{2,1,0:T(8,128)(2,1)}, bf16[2,128,3072]{2,1,0:T(8,128)(2,1)S(1)}, u32[]{:S(2)}, u32[]{:S(2)}) collective-permute-start(bf16[2,128,3072]{2,1,0:T(8,128)(2,1)} %dynamic-slice_bitcast_fusion.5), channel_id=1, source_target_pairs={{0,8},{1,9},{2,10},{3,11},{4,12},{5,13},{6,14},{7,15},{8,0},{9,1},... | collective-permute-start | bytes 4718600 | tf_op jit(solution)/shard_map/ppermute | solution.py:94
  470.9 36.8 %collective-permute-start.51 = (bf16[8,96,1024]{2,1,0:T(8,128)(2,1)}, bf16[8,96,1024]{2,1,0:T(8,128)(2,1)}, u32[]{:S(2)}, u32[]{:S(2)}) collective-permute-start(bf16[8,96,1024]{2,1,0:T(8,128)(2,1)} %dynamic-slice_bitcast_fusion.7), channel_id=1, source_target_pairs={{0,2},{1,3},{2,0},{3,1},{4,6},{5,7},{6,4},{7,5},{8,10},{9,11},{10,... | collective-permute-start | bytes 4718600 | tf_op jit(solution)/shard_map/ppermute | solution.py:94
  472.9 39.9 %collective-permute-start.52 = (bf16[4,64,3072]{2,1,0:T(8,128)(2,1)}, bf16[4,64,3072]{2,1,0:T(8,128)(2,1)}, u32[]{:S(2)}, u32[]{:S(2)}) collective-permute-start(bf16[4,64,3072]{2,1,0:T(8,128)(2,1)} %dynamic-slice_bitcast_fusion.6), channel_id=1, source_target_pairs={{0,4},{1,5},{2,6},{3,7},{4,0},{5,1},{6,2},{7,3},{8,12},{9,13},{10,... | collective-permute-start | bytes 4718600 | tf_op jit(solution)/shard_map/ppermute | solution.py:94
  572.8 39.5 %collective-permute-start.56 = (bf16[1,128,3072]{2,1,0:T(8,128)(2,1)}, bf16[1,128,3072]{2,1,0:T(8,128)(2,1)}, u32[]{:S(2)}, u32[]{:S(2)}) collective-permute-start(bf16[1,128,3072]{2,1,0:T(8,128)(2,1)} %dynamic-slice_bitcast_fusion.16), channel_id=1, source_target_pairs={{0,16},{1,17},{2,18},{3,19},{4,20},{5,21},{6,22},{7,23},{8,24},{9,... | collective-permute-start | bytes 2359304 | tf_op jit(solution)/shard_map/ppermute | solution.py:94
  576.8 36.8 %collective-permute-start.54 = (bf16[4,96,1024]{2,1,0:T(8,128)(2,1)}, bf16[4,96,1024]{2,1,0:T(8,128)(2,1)}, u32[]{:S(2)}, u32[]{:S(2)}) collective-permute-start(bf16[4,96,1024]{2,1,0:T(8,128)(2,1)} %dynamic-slice_bitcast_fusion.18), channel_id=1, source_target_pairs={{0,4},{1,5},{2,6},{3,7},{4,0},{5,1},{6,2},{7,3},{8,12},{9,13},{10,... | collective-permute-start | bytes 2359304 | tf_op jit(solution)/shard_map/ppermute | solution.py:94
  589.2 31.0 %collective-permute-start.57 = (bf16[16,64,1024]{2,1,0:T(8,128)(2,1)S(1)}, bf16[16,64,1024]{2,1,0:T(8,128)(2,1)S(1)}, u32[]{:S(2)}, u32[]{:S(2)}) collective-permute-start(bf16[16,64,1024]{2,1,0:T(8,128)(2,1)S(1)} %dynamic-slice_bitcast_fusion.4), channel_id=1, source_target_pairs={{0,1},{1,0},{2,3},{3,2},{4,5},{5,4},{6,7},{7,6},{8,9},{9,8},{10,11... | collective-permute-start | bytes 6291464 | tf_op jit(solution)/shard_map/ppermute | solution.py:94
  624.2 31.2 %collective-permute-start.58 = (bf16[2,96,1024]{2,1,0:T(8,128)(2,1)}, bf16[2,96,1024]{2,1,0:T(8,128)(2,1)}, u32[]{:S(2)}, u32[]{:S(2)}) collective-permute-start(bf16[2,96,1024]{2,1,0:T(8,128)(2,1)} %dynamic-slice_bitcast_fusion.25), channel_id=1, source_target_pairs={{0,8},{1,9},{2,10},{3,11},{4,12},{5,13},{6,14},{7,15},{8,0},{9,1},... | collective-permute-start | bytes 1179656 | tf_op jit(solution)/shard_map/ppermute | solution.py:94
  624.2 32.4 %collective-permute-start.59 = (bf16[1,64,3072]{2,1,0:T(8,128)(2,1)}, bf16[1,64,3072]{2,1,0:T(8,128)(2,1)}, u32[]{:S(2)}, u32[]{:S(2)}) collective-permute-start(bf16[1,64,3072]{2,1,0:T(8,128)(2,1)} %dynamic-slice_bitcast_fusion.24), channel_id=1, source_target_pairs={{0,16},{1,17},{2,18},{3,19},{4,20},{5,21},{6,22},{7,23},{8,24},{9,... | collective-permute-start | bytes 1179656 | tf_op jit(solution)/shard_map/ppermute | solution.py:94
  627.3 32.8 %collective-permute-start.61 = (bf16[8,64,1024]{2,1,0:T(8,128)(2,1)}, bf16[8,64,1024]{2,1,0:T(8,128)(2,1)}, u32[]{:S(2)}, u32[]{:S(2)}) collective-permute-start(bf16[8,64,1024]{2,1,0:T(8,128)(2,1)} %dynamic-slice_bitcast_fusion.15), channel_id=1, source_target_pairs={{0,2},{1,3},{2,0},{3,1},{4,6},{5,7},{6,4},{7,5},{8,10},{9,11},{10,... | collective-permute-start | bytes 3145736 | tf_op jit(solution)/shard_map/ppermute | solution.py:94
  665.8 34.2 %collective-permute-start.90 = (bf16[4,64,1024]{2,1,0:T(8,128)(2,1)}, bf16[4,64,1024]{2,1,0:T(8,128)(2,1)}, u32[]{:S(2)}, u32[]{:S(2)}) collective-permute-start(bf16[4,64,1024]{2,1,0:T(8,128)(2,1)} %dynamic-slice_bitcast_fusion.19), channel_id=1, source_target_pairs={{0,4},{1,5},{2,6},{3,7},{4,0},{5,1},{6,2},{7,3},{8,12},{9,13},{10,... | collective-permute-start | bytes 1572872 | tf_op jit(solution)/shard_map/ppermute | solution.py:94
  703.4 30.7 %collective-permute-start.80 = (bf16[16,32,1024]{2,1,0:T(8,128)(2,1)}, bf16[16,32,1024]{2,1,0:T(8,128)(2,1)}, u32[]{:S(2)}, u32[]{:S(2)}) collective-permute-start(bf16[16,32,1024]{2,1,0:T(8,128)(2,1)} %dynamic-slice_bitcast_fusion.9), channel_id=1, source_target_pairs={{0,1},{1,0},{2,3},{3,2},{4,5},{5,4},{6,7},{7,6},{8,9},{9,8},{10,11... | collective-permute-start | bytes 3145736 | tf_op jit(solution)/shard_map/ppermute | solution.py:94
  750.6 30.8 %collective-permute-start.76 = (bf16[4,64,2048]{2,1,0:T(8,128)(2,1)S(1)}, bf16[4,64,2048]{2,1,0:T(8,128)(2,1)S(1)}, u32[]{:S(2)}, u32[]{:S(2)}) collective-permute-start(bf16[4,64,2048]{2,1,0:T(8,128)(2,1)S(1)} %dynamic-slice_bitcast_fusion.10), channel_id=1, source_target_pairs={{0,4},{1,5},{2,6},{3,7},{4,0},{5,1},{6,2},{7,3},{8,12},{9,13},{10,... | collective-permute-start | bytes 3145736 | tf_op jit(solution)/shard_map/ppermute | solution.py:94
  (203 other events, 3130.2 us)
